TPU v7x, 32 devices: a whole 2x2x4 slice. The times are simulated.
32 devices in a mesh: ctx: 16 (over z, x, core), head: 2 (over y).
Axes of the slice: x: 2, y: 2, z: 4, core: 2. Of those that a mesh axis runs over, the one named last changes fastest.
Arguments:
- queries: bfloat16 [4096, 4, 8, 128], P('ctx', 'head'), may hold values from -6 to 6
- keys: bfloat16 [4096, 8, 128], P('ctx'), may hold values from -6 to 6
- values: bfloat16 [4096, 8, 128], P('ctx'), may hold values from -6 to 6
- dout: bfloat16 [4096, 4, 8, 128], P('ctx', 'head'), may hold values from -24 to 24
- signs: int32 [2, 128, 32], replicated, may hold values from 0 to 1
Outputs:
- dq: bfloat16 [4096, 4, 8, 128], P('ctx', 'head')
- dk: bfloat16 [4096, 8, 128], P('ctx', 'head')
- dv: bfloat16 [4096, 8, 128], P('ctx', 'head')
All inputs are finite; a program needn't handle non-finite values.
Results may differ from a plain program's by a relative error of at most 0.0075.
Values may be sent and summed in bfloat16 or wider, within the bound.
A program may use at most 128 MiB of HBM per device.

v0:
```python
import jax
import jax.numpy as jnp
from jax import lax
from jax.sharding import PartitionSpec as P

highest = lax.Precision.HIGHEST


def prefix(part, axis, combine, identity, reverse):
    count = lax.axis_size(axis)
    place = lax.axis_index(axis)
    ahead = count - 1 - place if reverse else place
    gathered = jax.tree.map(lambda a: lax.all_gather(a, axis), part)
    state = jax.tree.map(lambda a, e: jnp.zeros_like(a) + jnp.asarray(e, a.dtype), part, identity)

    def one(step, state):
        source = count - 1 - step if reverse else step
        return combine(
            state, jax.tree.map(lambda a: lax.dynamic_index_in_dim(a, source, 0, False), gathered)
        )

    return lax.fori_loop(0, ahead, one, state)


def sketch_parts(tokens, projector, pattern):
    inverse = tokens.shape[-1] ** (-0.5)
    sketch_one = (
        jnp.einsum(pattern, tokens, projector[0], preferred_element_type=jnp.float32) * inverse
    )
    sketch_two = (
        jnp.einsum(pattern, tokens, projector[1], preferred_element_type=jnp.float32) * inverse
    )
    return (sketch_one, sketch_two)


def features(sketch_one, sketch_two):
    width = sketch_one.shape[-1]
    sketch = sketch_one * sketch_two
    outer = sketch[..., :, None] * sketch[..., None, :] * (1.0 / width)
    return outer.reshape(sketch.shape[:-1] + (width * width,)).astype(jnp.bfloat16)


def feature_back(cotangent, sketch_one, sketch_two, proj_wide):
    width = sketch_one.shape[-1]
    sketch = sketch_one * sketch_two
    square = cotangent.reshape(cotangent.shape[:-1] + (width, width))
    dsketch = (
        jnp.einsum("...ab,...b->...a", square, sketch, precision=highest)
        + jnp.einsum("...ab,...a->...b", square, sketch, precision=highest)
    ) * (1.0 / width)
    back_one = jnp.einsum("...f,df->...d", dsketch * sketch_two, proj_wide[0], precision=highest)
    back_two = jnp.einsum("...f,df->...d", dsketch * sketch_one, proj_wide[1], precision=highest)
    return (back_one + back_two) * proj_wide.shape[1] ** (-0.5)


def head_step(inputs):
    key_feat, value_head, state_in, total_in, query_feat, grad_out = inputs
    length = key_feat.shape[0]
    causal = lax.broadcasted_iota(jnp.int32, (length, length), 0) >= lax.broadcasted_iota(
        jnp.int32, (length, length), 1
    )

    def member(query_one, grad_one):
        scores = jnp.where(
            causal,
            jnp.einsum("if,jf->ij", query_one, key_feat, preferred_element_type=jnp.float32),
            0.0,
        )
        weights = scores.astype(jnp.bfloat16)
        query_wide = query_one.astype(jnp.float32)
        numerator = jnp.dot(weights, value_head, preferred_element_type=jnp.float32) + jnp.dot(
            query_wide, state_in, precision=highest
        )
        denominator = 1.0 + jnp.sum(scores, 1) + jnp.dot(query_wide, total_in, precision=highest)
        output_rows = numerator / denominator[:, None]
        grad_rows = grad_one.astype(jnp.float32) / denominator[:, None]
        grad_low = grad_rows.astype(jnp.bfloat16)
        correction = -jnp.sum(grad_rows * output_rows, 1)
        dscores = jnp.where(
            causal,
            jnp.einsum("id,jd->ij", grad_low, value_head, preferred_element_type=jnp.float32)
            + correction[:, None],
            0.0,
        ).astype(jnp.bfloat16)
        grad_qfeat = (
            jnp.dot(dscores, key_feat, preferred_element_type=jnp.float32)
            + jnp.dot(grad_rows, state_in.T, precision=highest)
            + correction[:, None] * total_in[None, :]
        )
        grad_kfeat = jnp.einsum("ij,if->jf", dscores, query_one, preferred_element_type=jnp.float32)
        grad_value = jnp.einsum("ij,id->jd", weights, grad_low, preferred_element_type=jnp.float32)
        suffix_part = jnp.einsum(
            "if,id->fd", query_one, grad_low, preferred_element_type=jnp.float32
        )
        suffix_sum = jnp.dot(correction, query_wide, precision=highest)
        return (grad_qfeat, grad_kfeat, grad_value, suffix_part, suffix_sum)

    results = jax.vmap(member)(query_feat, grad_out)
    return (
        results[0],
        jnp.sum(results[1], 0),
        jnp.sum(results[2], 0),
        jnp.sum(results[3], 0),
        jnp.sum(results[4], 0),
    )


def add_states(earlier, later):
    return (earlier[0] + later[0], earlier[1] + later[1])


def prefix_scan(state, total):
    return prefix(
        (state, total), "ctx", add_states, (jnp.zeros_like(state), jnp.zeros_like(total)), False
    )


def suffix_scan(state, total):
    return prefix(
        (state, total), "ctx", add_states, (jnp.zeros_like(state), jnp.zeros_like(total)), True
    )


def later_terms(key_feat, value_heads, merged_state, merged_total):
    kfeat_extra = (
        jnp.einsum("htd,hfd->htf", value_heads.astype(jnp.float32), merged_state, precision=highest)
        + merged_total[:, None, :]
    )
    value_extra = jnp.einsum(
        "htf,hfd->htd", key_feat.astype(jnp.float32), merged_state, precision=highest
    )
    return (kfeat_extra, value_extra)


def body(queries, keys, values, dout, signs):
    projector = (2 * signs - 1).astype(jnp.bfloat16)
    proj_wide = projector.astype(jnp.float32)
    heads_all = keys.shape[1]
    owned = heads_all // lax.axis_size("head")
    offset = lax.axis_index("head") * owned
    key_part = lax.dynamic_slice_in_dim(keys, offset, owned, 1)
    value_part = lax.dynamic_slice_in_dim(values, offset, owned, 1)
    query_part, grad_part = (
        lax.all_to_all(queries, "head", split_axis=2, concat_axis=1, tiled=True),
        lax.all_to_all(dout, "head", split_axis=2, concat_axis=1, tiled=True),
    )
    key_one, key_two = sketch_parts(key_part, projector, "thd,df->htf")
    key_feat = features(key_one, key_two)
    query_one, query_two = sketch_parts(query_part, projector, "tmhd,df->hmtf")
    query_feat = features(query_one, query_two)
    value_heads = value_part.transpose(1, 0, 2)
    grad_heads = grad_part.transpose(2, 1, 0, 3)
    block_state = jnp.einsum(
        "htf,htd->hfd", key_feat, value_heads, preferred_element_type=jnp.float32
    )
    block_total = jnp.sum(key_feat, 1, dtype=jnp.float32)
    state_in, total_in = prefix_scan(block_state, block_total)
    grad_qfeat, grad_kfeat, grad_value, suffix_part, suffix_sum = lax.map(
        head_step, (key_feat, value_heads, state_in, total_in, query_feat, grad_heads)
    )
    query_grad = feature_back(grad_qfeat, query_one, query_two, proj_wide)
    query_low = query_grad.transpose(2, 1, 0, 3).astype(jnp.bfloat16)
    query_out = lax.all_to_all(query_low, "head", split_axis=1, concat_axis=2, tiled=True)
    merged_state, merged_total = suffix_scan(suffix_part, suffix_sum)
    kfeat_extra, value_extra = later_terms(key_feat, value_heads, merged_state, merged_total)
    key_sum = feature_back(grad_kfeat + kfeat_extra, key_one, key_two, proj_wide)
    value_sum = grad_value + value_extra
    key_out = key_sum.transpose(1, 0, 2).astype(jnp.bfloat16)
    value_out = value_sum.transpose(1, 0, 2).astype(jnp.bfloat16)
    return (query_out, key_out, value_out)


def solution(mesh):
    in_specs = (
        P("ctx", "head", None, None),
        P("ctx", None, None),
        P("ctx", None, None),
        P("ctx", "head", None, None),
        P(),
    )
    out_specs = (P("ctx", "head", None, None), P("ctx", "head", None), P("ctx", "head", None))
    return jax.shard_map(body, mesh=mesh, in_specs=in_specs, out_specs=out_specs, check_vma=False)
```

profile of v0, /device:TPU:0, one launch (start us, length us, event | category | flops | bytes accessed | tf_op | source)
XLA Modules:
  0.0 605.0 jit_solution(9288683914264486914)
XLA Ops:
  14.7 4.2 all-to-all-start.1
  21.4 12.0 %all-to-all-done.1 = bf16[256,2,8,128]{3,0,1,2:T(8,128)(2,1)S(1)} async-done(((bf16[256,2,8,128]{3,0,1,2:T(8,128)(2,1)}), bf16[256,2,8,128]{3,0,1,2:T(8,128)(2,1)S(1)}, u32[]{:S(2)}, u32[]{:S(2)}) %all-to-all-start.1) | async-done | bytes 1048608 | tf_op jit(solution)/shard_map/all_to_all | solution.py:144
  33.4 4.4 all-to-all-start
  38.7 24.0 %all_gather.27 = f32[16,4,1024]{2,1,0:T(4,128)S(1)} all-gather(f32[1,4,1024]{2,1,0:T(4,128)S(1)} %all_gather.26), channel_id=1, replica_groups=mesh['ctx'=16,'head'=2] {'ctx'}, dimensions={0}, use_global_device_ids=true | all-gather | bytes 278528 | tf_op jit(solution)/shard_map/all_gather | solution.py:13
  66.8 6.3 %multiply_convert_fusion = bf16[4,4,256,32,32]{2,4,3,1,0:T(8,128)(2,1)} fusion(f32[4,4,256,32]{2,3,0,1:T(8,128)S(1)} %get-tuple-element.309), kind=kLoop, calls=%fused_computation.84 | loop fusion | flops 12582912 | bytes 8912896 | tf_op jit(solution)/shard_map/convert_element_type | solution.py:40
  73.2 113.3 %all-gather.7.cloned.1.call-done = f32[64,1024,128]{2,1,0:T(8,128)} async-done(((f32[4,1024,128]{2,1,0:T(8,128)}), f32[64,1024,128]{2,1,0:T(8,128)}) %all-gather.7.cloned.1.call-update) | async-done | bytes 33554448 | tf_op jit(solution)/shard_map/all_gather | solution.py:13
  188.9 155.5 %while.45 = (s32[]{:T(128)}, f32[4,4,256,1024]{2,3,1,0:T(8,128)}, f32[4,256,1024]{2,1,0:T(8,128)}, f32[4,256,128]{2,1,0:T(8,128)}, f32[4,1024,128]{2,1,0:T(8,128...) while((s32[]{:T(128)}, f32[4,4,256,1024]{2,3,1,0:T(8,128)}, ...), condition=%wide.region_6.7_spmd, body=%wide.region_3.6_spmd.sunk | while | flops 5333779456 | bytes 61172536 | solution.py:158
  188.9 2.5 fusion.197
  194.3 2.8 fusion.200
  199.8 5.8 add_bitcast_fusion.2
  205.6 5.4 copy.217
  211.0 4.7 constant_dynamic-update-slice_fusion.2
  215.7 3.3 fusion.203
  219.1 3.1 fusion.205
  223.1 3.3 fusion.206
  227.8 2.5 fusion.197
  233.2 2.8 fusion.200
  238.7 5.8 add_bitcast_fusion.2
  244.5 5.4 copy.217
  249.9 4.6 constant_dynamic-update-slice_fusion.2
  254.6 3.3 fusion.203
  257.9 3.1 fusion.205
  262.0 3.3 fusion.206
  266.7 2.5 fusion.197
  272.1 2.8 fusion.200
  277.6 5.8 add_bitcast_fusion.2
  283.4 5.4 copy.217
  288.8 4.6 constant_dynamic-update-slice_fusion.2
  293.4 3.3 fusion.203
  296.7 3.1 fusion.205
  300.7 3.3 fusion.206
  310.8 2.8 fusion.200
  316.3 5.8 add_bitcast_fusion.2
  322.2 5.4 copy.217
  327.5 4.6 constant_dynamic-update-slice_fusion.2
  332.1 3.3 fusion.203
  335.4 3.1 fusion.205
  339.5 3.3 fusion.206
  344.4 9.6 %multiply_reduce_fusion.1 = f32[4,4,256,32]{2,3,1,0:T(8,128)S(1)} fusion(f32[4,4,256,1024]{2,3,1,0:T(8,128)} %get-tuple-element.186, f32[4,4,256,32]{2,3,0,1:T(8,128)} %copy-done.4), kind=kLoop, calls=%fused_computation.83 | loop fusion | flops 8257536 | bytes 17825792
  354.1 8.9 %multiply_reduce_fusion = f32[4,4,256,32]{2,3,1,0:T(8,128)S(1)} fusion(f32[4,4,256,32,32]{2,4,3,1,0:T(8,128)} %bitcast.282, f32[4,4,256,32]{2,3,0,1:T(8,128)S(1)} %copy-done.5), kind=kLoop, calls=%fused_computation.82 | loop fusion | flops 8257536 | bytes 17825792
  367.9 3.6 all-to-all-start.2
  371.5 52.7 %all-gather.3 = f32[16,4,1024]{2,1,0:T(4,128)S(1)} all-gather(f32[1,4,1024]{2,1,0:T(4,128)S(1)} %bitcast.296), channel_id=4, replica_groups=mesh['ctx'=16,'head'=2] {'ctx'}, dimensions={0}, use_global_device_ids=true | all-gather | bytes 278528 | tf_op jit(solution)/shard_map/all_gather | solution.py:13
  425.9 119.8 %all-gather.9.cloned.1.call-done = f32[64,1024,128]{2,1,0:T(8,128)} async-done(((f32[4,1024,128]{2,1,0:T(8,128)}), f32[64,1024,128]{2,1,0:T(8,128)}) %all-gather.9.cloned.1.call-update) | async-done | bytes 33554448 | tf_op jit(solution)/shard_map/all_gather | solution.py:13
  545.9 31.2 %while.46 = (s32[]{:T(128)}, f32[4,1024,128]{2,1,0:T(8,128)S(1)}, f32[4,1024]{1,0:T(4,128)S(1)}, s32[]{:T(128)}, f32[16,4,1024,128]{3,2,1,0:T(8,128)}, /*index=5...) while((s32[]{:T(128)}, f32[4,1024,128]{2,1,0:T(8,128)S(1)}, ...), condition=%wide.region_8.9_spmd, body=%wide.region_7.8_spmd.sunk | while | flops 528390 | bytes 6340763 | solution.py:22
  577.1 3.9 fusion.97
  581.9 4.2 add_add_fusion
  586.1 5.4 copy.162
  591.5 3.2 multiply_reduce_fusion.3
  (198 shorter events, 92.8 us)
Async XLA Ops:
  7.2 1.1 copy-start
  7.2 2.9 copy-start.23
  7.2 179.3 %all-gather.7.cloned.1.call-start = ((), (), s32[]{:S(2)}) async-start(), calls=%async_computation.3 | async-start | bytes 35651584 | tf_op jit(solution)/shard_map/all_gather | solution.py:13
  8.1 57.5 %copy-start.20 = (bf16[2,128,32]{1,2,0:T(8,128)(2,1)}, bf16[2,128,32]{1,2,0:T(8,128)(2,1)S(1)}, u32[]{:S(2)}) copy-start(bf16[2,128,32]{1,2,0:T(8,128)(2,1)S(1)} %add_convert_fusion) | copy-start | bytes 49156
  8.5 4.9 copy-start.13
  9.4 4.1 copy-start.15
  10.1 1.3 copy-start.2
  14.7 18.7 %all-to-all-start.1 = ((bf16[256,2,8,128]{3,0,1,2:T(8,128)(2,1)}), bf16[256,2,8,128]{3,0,1,2:T(8,128)(2,1)S(1)}, u32[]{:S(2)}, u32[]{:S(2)}) async-start(bf16[256,2,8,128]{3,0,1,2:T(8,128)(2,1)} %copy.102), calls=%async_computation.1 | async-start | bytes 2097152 | tf_op jit(solution)/shard_map/all_to_all | solution.py:144
  33.4 29.4 %all-to-all-start = ((bf16[256,2,8,128]{3,0,1,2:T(8,128)(2,1)}), bf16[256,2,8,128]{3,0,1,2:T(8,128)(2,1)}, u32[]{:S(2)}, u32[]{:S(2)}) async-start(bf16[256,2,8,128]{3,0,1,2:T(8,128)(2,1)} %copy.100), calls=%async_computation | async-start | bytes 2097152 | tf_op jit(solution)/shard_map/all_to_all | solution.py:145
  37.8 507.9 %all-gather.9.cloned.1.call-start = ((), (), s32[]{:S(2)}) async-start(), calls=%async_computation.4 | async-start | bytes 35651584 | tf_op jit(solution)/shard_map/all_gather | solution.py:13
  65.6 1.3 copy-start.8
  66.8 6.3 %copy-start.4 = (f32[4,4,256,32]{2,3,0,1:T(8,128)}, f32[4,4,256,32]{2,3,0,1:T(8,128)S(1)}, u32[]{:S(2)}) copy-start(f32[4,4,256,32]{2,3,0,1:T(8,128)S(1)} %get-tuple-element.309) | copy-start | bytes 1572868
  188.9 5.1 copy-start.12
  188.9 5.4 copy-start.6
  194.0 5.8 copy-start.18
  211.0 8.0 %copy-start.7 = (bf16[4,4,256,128]{2,3,1,0:T(8,128)(2,1)S(1)}, bf16[4,4,256,128]{2,3,1,0:T(8,128)(2,1)}, u32[]{:S(2)}) copy-start(bf16[4,4,256,128]{2,3,1,0:T(8,128)(2,1)} %get-tuple-element.533) | copy-start | bytes 3145732 | tf_op jit(solution)/shard_map/while
  211.0 8.0 %copy-start.19 = (f32[4,256]{1,0:T(4,128)S(1)}, f32[4,256]{1,0:T(4,128)}, u32[]{:S(2)}) copy-start(f32[4,256]{1,0:T(4,128)} %copy-done.18) | copy-start | bytes 12292 | tf_op jit(solution)/shard_map/while
  219.1 4.1 copy-start.22
  227.8 5.1 copy-start.12
  227.8 5.4 copy-start.6
  232.9 5.8 copy-start.18
  249.9 8.0 %copy-start.7 = (bf16[4,4,256,128]{2,3,1,0:T(8,128)(2,1)S(1)}, bf16[4,4,256,128]{2,3,1,0:T(8,128)(2,1)}, u32[]{:S(2)}) copy-start(bf16[4,4,256,128]{2,3,1,0:T(8,128)(2,1)} %get-tuple-element.533) | copy-start | bytes 3145732 | tf_op jit(solution)/shard_map/while
  249.9 8.0 %copy-start.19 = (f32[4,256]{1,0:T(4,128)S(1)}, f32[4,256]{1,0:T(4,128)}, u32[]{:S(2)}) copy-start(f32[4,256]{1,0:T(4,128)} %copy-done.18) | copy-start | bytes 12292 | tf_op jit(solution)/shard_map/while
  257.9 4.1 copy-start.22
  266.6 5.1 copy-start.12
  266.6 5.4 copy-start.6
  271.8 5.8 copy-start.18
  288.8 7.9 %copy-start.7 = (bf16[4,4,256,128]{2,3,1,0:T(8,128)(2,1)S(1)}, bf16[4,4,256,128]{2,3,1,0:T(8,128)(2,1)}, u32[]{:S(2)}) copy-start(bf16[4,4,256,128]{2,3,1,0:T(8,128)(2,1)} %get-tuple-element.533) | copy-start | bytes 3145732 | tf_op jit(solution)/shard_map/while
  288.8 7.9 %copy-start.19 = (f32[4,256]{1,0:T(4,128)S(1)}, f32[4,256]{1,0:T(4,128)}, u32[]{:S(2)}) copy-start(f32[4,256]{1,0:T(4,128)} %copy-done.18) | copy-start | bytes 12292 | tf_op jit(solution)/shard_map/while
  296.6 4.1 copy-start.22
  305.4 5.1 copy-start.12
  305.4 5.4 copy-start.6
  310.5 5.8 copy-start.18
  327.5 7.9 %copy-start.7 = (bf16[4,4,256,128]{2,3,1,0:T(8,128)(2,1)S(1)}, bf16[4,4,256,128]{2,3,1,0:T(8,128)(2,1)}, u32[]{:S(2)}) copy-start(bf16[4,4,256,128]{2,3,1,0:T(8,128)(2,1)} %get-tuple-element.533) | copy-start | bytes 3145732 | tf_op jit(solution)/shard_map/while
  327.5 7.9 %copy-start.19 = (f32[4,256]{1,0:T(4,128)S(1)}, f32[4,256]{1,0:T(4,128)}, u32[]{:S(2)}) copy-start(f32[4,256]{1,0:T(4,128)} %copy-done.18) | copy-start | bytes 12292 | tf_op jit(solution)/shard_map/while
  335.4 4.1 copy-start.22
  344.4 9.6 %copy-start.5 = (f32[4,4,256,32]{2,3,0,1:T(8,128)S(1)}, f32[4,4,256,32]{2,3,0,1:T(8,128)}, u32[]{:S(2)}) copy-start(f32[4,4,256,32]{2,3,0,1:T(8,128)} %copy-done.4) | copy-start | bytes 1572868
  354.0 8.9 %copy-start.9 = (f32[4,4,256,32]{2,3,0,1:T(8,128)S(1)}, f32[4,4,256,32]{2,3,0,1:T(8,128)}, u32[]{:S(2)}) copy-start(f32[4,4,256,32]{2,3,0,1:T(8,128)} %copy-done.8) | copy-start | bytes 1572868
  354.0 8.9 %copy-start.11 = (f32[4,4,256,32]{2,3,0,1:T(8,128)S(1)}, f32[4,4,256,32]{2,3,0,1:T(8,128)}, u32[]{:S(2)}) copy-start(f32[4,4,256,32]{2,3,0,1:T(8,128)} %get-tuple-element.310) | copy-start | bytes 1572868
  354.1 9.1 %copy-start.21 = (bf16[2,128,32]{1,2,0:T(8,128)(2,1)S(1)}, bf16[2,128,32]{1,2,0:T(8,128)(2,1)}, u32[]{:S(2)}) copy-start(bf16[2,128,32]{1,2,0:T(8,128)(2,1)} %copy-done.20) | copy-start | bytes 49156
  365.0 6.5 %copy-start.24 = (f32[4,1024]{1,0:T(4,128)S(1)}, f32[4,1024]{1,0:T(4,128)}, u32[]{:S(2)}) copy-start(f32[4,1024]{1,0:T(4,128)} %get-tuple-element.189) | copy-start | bytes 49156
  367.9 56.3 %all-to-all-start.2 = ((bf16[256,4,4,128]{3,0,2,1:T(8,128)(2,1)}), bf16[256,4,4,128]{3,0,2,1:T(8,128)(2,1)S(1)}, u32[]{:S(2)}, u32[]{:S(2)}) async-start(bf16[256,4,4,128]{3,0,2,1:T(8,128)(2,1)} %copy.114), calls=%async_computation.2 | async-start | bytes 2097152 | tf_op jit(solution)/shard_map/all_to_all | solution.py:163
  545.9 31.2 %copy-start.16 = (f32[4,256,128]{2,1,0:T(8,128)S(1)}, f32[4,256,128]{2,1,0:T(8,128)}, u32[]{:S(2)}) copy-start(f32[4,256,128]{2,1,0:T(8,128)} %get-tuple-element.192) | copy-start | bytes 1572868
  577.1 4.8 copy-start.10
  591.5 3.4 copy-start.3
  591.5 4.1 copy-start.14
  591.5 4.7 copy-start.17
  591.5 6.2 %copy-start.1 = (bf16[256,8,128]{2,1,0:T(8,128)(2,1)S(1)}, bf16[256,8,128]{2,1,0:T(8,128)(2,1)}, u32[]{:S(2)}) copy-start(bf16[256,8,128]{2,1,0:T(8,128)(2,1)} %param.12) | copy-start | bytes 1572868
Sparse Core Ops, SparseCore 0:
  13.6 172.8 all-gather.6
  344.5 201.1 all-gather.8
where the time goes:
time: 613 us; the launch traced here: 605 us
  waiting for transfers between devices  245 us (40%)
  matrix products  124 us (20%)
  blocking collectives  76.7 us (13%)
  local copies, waits for them, and re-layouts  66.8 us (11%)
  other arithmetic  63.5 us (10%)
  between operations  14.9 us (2%)
  starting transfers between devices  12.3 us (2%)
    all_gather x2, waiting for transfers between devices, prefix(): gathered = jax.tree.map(lambda a: lax.all_gather(a, axis), part)  233 us
    all_gather x2, blocking collectives, prefix(): gathered = jax.tree.map(lambda a: lax.all_gather(a, axis), part)  76.7 us
    dynamic_update_slice x12, local copies, waits for them, and re-layouts, body(): lax.map(head_step, (key_feat, value_heads, state_in, total_in, query_feat...  45.5 us
    add x30, other arithmetic, add_states(): return (earlier[0] + later[0], earlier[1] + later[1])  30.7 us
    dot_general x4, matrix products, member(): jnp.dot(grad_rows, state_in.T, precision=highest)  23.3 us
    unnamed x2, other arithmetic  18.5 us
    unnamed x44, local copies, waits for them, and re-layouts  13.3 us
    dot_general x4, matrix products, member(): jnp.einsum('ij,if->jf', dscores, query_one, preferred_element_type=jnp.fl...  13.2 us
  transfers between devices with their start and end apart: 5, of which 3 were waited for; matrix products, arithmetic and copies ran while one was open for 7% of the time, Pallas kernels for 0%

commit v1 on v0

v1 whole, which is shorter than its diff:
```python
import jax
import jax.numpy as jnp
from jax import lax
from jax.experimental import pallas as pl
from jax.experimental.pallas import tpu as pltpu
from jax.sharding import PartitionSpec as P

f32 = jnp.float32
bf16 = jnp.bfloat16
GRANT = 56 * 1024 * 1024


def dot(first, second, dims):
    return lax.dot_general(first, second, (dims, ((), ())), preferred_element_type=f32)


def nn(first, second):
    return dot(first, second, ((1,), (0,)))


def nt(first, second):
    return dot(first, second, ((1,), (1,)))


def pair_count(width):
    return width * width // 2 + width // 2


def sketches(tokens, proj, width):
    both = dot(proj, tokens, ((0,), (1,))) * tokens.shape[-1] ** (-0.5)
    return both[:width], both[width:]


def pair_features(s):
    width = s.shape[0]
    half = width // 2
    scaled = s * (1.0 / width)
    parts = [(scaled * s).astype(bf16)]
    for d in range(1, half):
        parts.append((scaled * pltpu.roll(s, width - d, 0)).astype(bf16))
    parts.append((scaled[:half] * s[half:]).astype(bf16))
    return jnp.concatenate(parts, axis=0)


def pair_back(c, s):
    width = s.shape[0]
    half = width // 2
    acc = c[:width] * s
    for d in range(1, half):
        one = c[d * width : (d + 1) * width]
        acc = acc + one * pltpu.roll(s, width - d, 0) + pltpu.roll(one * s, d, 0)
    last = c[half * width :]
    acc = acc + jnp.concatenate([last * s[half:], last * s[:half]], axis=0)
    return acc * (2.0 / width)


def doubled(rows, width, axis):
    place = lax.broadcasted_iota(jnp.int32, rows.shape, axis)
    return jnp.where(place < width, rows, rows * 2.0)


def split(a):
    high = a.astype(bf16)
    return high, (a - high.astype(f32)).astype(bf16)


def finish(ds, one, two, proj, scale):
    high, low = split(jnp.concatenate([ds * two, ds * one], axis=0))
    both = jnp.concatenate([proj, proj], axis=1)
    return dot(jnp.concatenate([high, low], axis=0), both, ((0,), (1,))) * scale


def pack_totals(column, lanes):
    count = column.shape[0]
    row = column.T[:1]
    rows = []
    for start in range(0, count, lanes):
        piece = row[:, start : start + lanes]
        if piece.shape[1] < lanes:
            piece = jnp.concatenate(
                [piece, jnp.zeros((1, lanes - piece.shape[1]), f32)], axis=1
            )
        rows.append(piece)
    rows.append(jnp.zeros((16 - len(rows), lanes), f32))
    return jnp.concatenate(rows, axis=0)


def unpack_totals(packed, count):
    lanes = packed.shape[1]
    parts = [packed[k : k + 1] for k in range(-(-count // lanes))]
    return jnp.concatenate(parts, axis=1)[:, :count]


def ones_beside(v):
    lane = lax.broadcasted_iota(jnp.int32, v.shape, 1)
    return jnp.concatenate([v, jnp.where(lane == 0, 1.0, 0.0).astype(bf16)], axis=1)


def state_with_totals(wide, lanes):
    return jnp.concatenate([wide[:, :lanes], pack_totals(wide[:, lanes:], lanes)], axis=0)


def first_kernel(q_ref, k_ref, v_ref, proj_ref, s_ref, state_ref):
    proj = proj_ref[...]
    width = proj.shape[1] // 2

    @pl.loop(0, k_ref.shape[0])
    def _(h):
        one, two = sketches(k_ref[h], proj, width)
        feat = pair_features((one * two).astype(bf16).astype(f32))
        v = v_ref[h]
        wide = nn(feat, ones_beside(v))
        state_ref[h] = state_with_totals(wide, v.shape[1]).astype(bf16)

    @pl.loop(0, q_ref.shape[0])
    def _(m):
        @pl.loop(0, q_ref.shape[1])
        def _(h):
            one, two = sketches(q_ref[m, h], proj, width)
            s_ref[m, h] = (one * two).astype(bf16)


def main_kernel(
    sq_ref, k_ref, v_ref, g_ref, proj_ref, state_ref, dsq_ref, dsk_ref, dv_ref, out_ref
):
    proj = proj_ref[...]
    width = proj.shape[1] // 2
    pairs = pair_count(width)
    members = sq_ref.shape[0]
    tokens, lanes = v_ref.shape[1:]
    one, two = sketches(k_ref[0], proj, width)
    skt = (one * two).astype(bf16)
    sk = (one * two).T.astype(bf16)
    v = v_ref[0]
    sqt = jnp.concatenate([sq_ref[m, 0] for m in range(members)], axis=1)
    sq = sqt.astype(f32)
    gout = jnp.concatenate([g_ref[m, 0].astype(f32).T for m in range(members)], axis=1)
    feat = pair_features(sq)
    state = state_ref[0][:pairs]
    totals = unpack_totals(state_ref[0][pairs:], pairs)

    inside = nn(sk, sqt)
    row = lax.broadcasted_iota(jnp.int32, inside.shape, 0)
    column = lax.rem(lax.broadcasted_iota(jnp.int32, inside.shape, 1), tokens)
    inside = jnp.where(row <= column, inside, 0.0)
    weights = (inside * inside * (1.0 / width**2)).astype(bf16)
    left = jnp.concatenate([v.astype(f32).T, jnp.ones((8, tokens), f32)], axis=0).astype(bf16)
    total_high = totals.astype(bf16).astype(f32)
    total_rows = jnp.concatenate(
        [total_high, totals - total_high, jnp.zeros((6, pairs), f32)], axis=0
    )
    state_rows = doubled(jnp.concatenate([state.T, total_rows], axis=0), width, 1).astype(bf16)
    over = nn(left, weights) + nn(state_rows, feat)
    low_total = nn(state_rows[lanes:], feat)[1:2]
    scale = 1.0 / (1.0 + over[lanes : lanes + 1] + low_total)
    rows = gout * scale
    correction = -jnp.sum(rows * over[:lanes], axis=0, keepdims=True) * scale
    low = rows.astype(bf16)
    dscores = nn(v, low) + correction
    edge = (dscores * inside * (2.0 / width**2)).astype(bf16)
    dsk_ref[0] = nt(edge, sqt)
    dv_ref[0] = nt(weights, low)

    corr_high = correction.astype(bf16).astype(f32)
    corr_rows = jnp.concatenate(
        [corr_high, correction - corr_high, jnp.zeros((lanes - 2, sq.shape[1]), f32)], axis=0
    ).astype(bf16)
    spread = jnp.concatenate([low, corr_rows], axis=0)
    total_columns = jnp.concatenate(
        [totals, totals, jnp.zeros((lanes - 2, pairs), f32)], axis=0
    ).T
    cotangent = nn(jnp.concatenate([state, total_columns], axis=1).astype(bf16), spread)
    dsq = nn(skt, edge) + pair_back(cotangent, sq)
    for m in range(members):
        dsq_ref[m, 0] = dsq[:, m * tokens : (m + 1) * tokens].astype(bf16)

    wide = nt(feat, spread)
    both = wide[:, lanes:] + pltpu.roll(wide[:, lanes:], lanes - 1, 1)
    out_ref[0] = state_with_totals(jnp.concatenate([wide[:, :lanes], both], axis=1), lanes).astype(
        bf16
    )


def last_kernel(
    q_ref, ds_ref, k_ref, v_ref, proj_ref, state_ref, dsk_ref, dv_ref, dq_ref, dk_ref, dvo_ref
):
    proj = proj_ref[...]
    width = proj.shape[1] // 2
    pairs = pair_count(width)
    inverse = k_ref.shape[-1] ** (-0.5)

    @pl.loop(0, k_ref.shape[0])
    def _(h):
        one, two = sketches(k_ref[h], proj, width)
        s = (one * two).astype(bf16).astype(f32)
        feat = pair_features(s)
        v = v_ref[h]
        lanes = v.shape[1]
        state = state_ref[h][:pairs]
        totals = unpack_totals(state_ref[h][pairs:], pairs)
        total_columns = jnp.concatenate([totals, jnp.zeros((lanes - 1, pairs), f32)], axis=0).T
        cotangent = nt(
            jnp.concatenate([state, total_columns], axis=1).astype(bf16), ones_beside(v)
        )
        ds = dsk_ref[h].T + pair_back(cotangent, s)
        dk_ref[h] = finish(ds, one, two, proj, inverse).astype(bf16)
        state_rows = doubled(state.T, width, 1).astype(bf16)
        dvo_ref[h] = (dv_ref[h] + nn(state_rows, feat).T).astype(bf16)

    @pl.loop(0, q_ref.shape[0])
    def _(m):
        @pl.loop(0, q_ref.shape[1])
        def _(h):
            one, two = sketches(q_ref[m, h], proj, width)
            ds = ds_ref[m, h].astype(f32)
            dq_ref[m, h] = finish(ds, one, two, proj, inverse).astype(bf16)


def call(kernel, outs, args, **more):
    return pl.pallas_call(
        kernel,
        out_shape=outs,
        compiler_params=pltpu.CompilerParams(vmem_limit_bytes=GRANT),
        **more,
    )(*args)


def body(queries, keys, values, dout, signs):
    proj = jnp.concatenate([2 * signs[0] - 1, 2 * signs[1] - 1], axis=1).astype(bf16)
    width = signs.shape[-1]
    pairs = pair_count(width)
    rows = pairs + 16
    heads_all = keys.shape[1]
    owned = heads_all // lax.axis_size("head")
    offset = lax.axis_index("head") * owned
    k = lax.dynamic_slice_in_dim(keys, offset, owned, 1).transpose(1, 0, 2)
    v = lax.dynamic_slice_in_dim(values, offset, owned, 1).transpose(1, 0, 2)
    q = queries.transpose(1, 2, 0, 3)
    g = dout.transpose(1, 2, 0, 3)
    mine, _, tokens, hd = q.shape
    members = mine * lax.axis_size("head")
    shape = jax.ShapeDtypeStruct
    sq, block_state = call(
        first_kernel,
        (shape((mine, heads_all, width, tokens), bf16), shape((owned, rows, hd), bf16)),
        (q, k, v, proj),
    )
    sq = lax.all_to_all(sq, "head", split_axis=1, concat_axis=0, tiled=True)
    g = lax.all_to_all(g, "head", split_axis=1, concat_axis=0, tiled=True)
    count = lax.axis_size("ctx")
    place = lax.axis_index("ctx")
    source = lax.broadcasted_iota(jnp.int32, (count, 1, 1, 1), 0)

    def scan(part, keep):
        gathered = lax.all_gather(part, "ctx")
        return jnp.sum(jnp.where(keep, gathered.astype(f32), 0.0), 0)

    state = scan(block_state, source < place)
    by_member = lambda h: (0, h, 0, 0)
    by_head = lambda h: (h, 0, 0)
    dsq, dsk, dv, part = call(
        main_kernel,
        (
            shape((members, owned, width, tokens), bf16),
            shape((owned, tokens, width), f32),
            shape((owned, tokens, hd), f32),
            shape((owned, rows, hd), bf16),
        ),
        (sq, k, v, g, proj, state),
        grid=(owned,),
        in_specs=[
            pl.BlockSpec((members, 1, width, tokens), by_member),
            pl.BlockSpec((1, tokens, hd), by_head),
            pl.BlockSpec((1, tokens, hd), by_head),
            pl.BlockSpec((members, 1, tokens, hd), by_member),
            pl.BlockSpec((hd, 2 * width), lambda h: (0, 0)),
            pl.BlockSpec((1, rows, hd), by_head),
        ],
        out_specs=(
            pl.BlockSpec((members, 1, width, tokens), by_member),
            pl.BlockSpec((1, tokens, width), by_head),
            pl.BlockSpec((1, tokens, hd), by_head),
            pl.BlockSpec((1, rows, hd), by_head),
        ),
    )
    dsq = lax.all_to_all(dsq, "head", split_axis=0, concat_axis=1, tiled=True)
    later = scan(part, source > place)
    dq, dk, dv = call(
        last_kernel,
        (
            shape((mine, heads_all, tokens, hd), bf16),
            shape((owned, tokens, hd), bf16),
            shape((owned, tokens, hd), bf16),
        ),
        (q, dsq, k, v, proj, later, dsk, dv),
    )
    return dq.transpose(2, 0, 1, 3), dk.transpose(1, 0, 2), dv.transpose(1, 0, 2)


def solution(mesh):
    in_specs = (
        P("ctx", "head", None, None),
        P("ctx", None, None),
        P("ctx", None, None),
        P("ctx", "head", None, None),
        P(),
    )
    out_specs = (P("ctx", "head", None, None), P("ctx", "head", None), P("ctx", "head", None))
    return jax.shard_map(body, mesh=mesh, in_specs=in_specs, out_specs=out_specs, check_vma=False)
```

time: 613 us -> 230 us (0.38); the launches traced: 605 us -> 229 us
  matrix products: 124 us -> 0 us
  waiting for transfers between devices: 245 us -> 139 us
  blocking collectives: 76.7 us -> 0 us
  other arithmetic: 63.5 us -> 13.6 us
  local copies, waits for them, and re-layouts: 66.8 us -> 20.3 us
  Pallas kernels: 0 us -> 31 us
    dot_general x55 -> x0, matrix products: 124 us -> none  [the longest x4 23.3 us: member(): jnp.dot(grad_rows, state_in.T, precision=highest)]
    all_gather x2, waiting for transfers between devices: 233 us -> 118 us  [scan(): gathered = lax.all_gather(part, 'ctx')]
    all_gather x2 -> x0, blocking collectives: 76.7 us -> none  [prefix(): gathered = jax.tree.map(lambda a: lax.all_gather(a, axis), part)]
    dynamic_update_slice x12 -> x0, local copies, waits for them, and re-layouts: 45.5 us -> none  [body(): lax.map(head_step, (key_feat, value_heads, state_in, total_in, query_feat...]
    pallas_call x0 -> x3, Pallas kernels: none -> 31 us  [call(): pl.pallas_call(kernel, out_shape=outs, compiler_params=pltpu.CompilerPara...]
    add x34 -> x0, other arithmetic: 30.7 us -> none  [the longest x30 30.7 us: add_states(): return (earlier[0] + later[0], earlier[1] + later[1])]
    unnamed x2 -> x0, other arithmetic: 18.5 us -> none
    reduce_sum x1 -> x2, other arithmetic: 0.66 us -> 12.9 us  [scan(): return jnp.sum(jnp.where(keep, gathered.astype(f32), 0.0), 0)]
  transfers between devices with their start and end apart: 5 -> 5, of which waited for: 3 -> 5; matrix products, arithmetic and copies ran while one was open for 7% -> 3% of each run, Pallas kernels for 0% -> 0%
where the time goes in v1:
time: 230 us; the launch traced here: 229 us
  waiting for transfers between devices  139 us (60%)
  Pallas kernels  31 us (13%)
  local copies, waits for them, and re-layouts  20.3 us (9%)
  between operations  14.1 us (6%)
  other arithmetic  13.6 us (6%)
  starting transfers between devices  11.3 us (5%)
    all_gather x2, waiting for transfers between devices, scan(): gathered = lax.all_gather(part, 'ctx')  118 us
    pallas_call x3, Pallas kernels, call(): pl.pallas_call(kernel, out_shape=outs, compiler_params=pltpu.CompilerPara...  31 us
    unnamed x9, local copies, waits for them, and re-layouts  13.7 us
    reduce_sum x2, other arithmetic, scan(): return jnp.sum(jnp.where(keep, gathered.astype(f32), 0.0), 0)  12.9 us
    all_to_all x1, waiting for transfers between devices, body(): g = lax.all_to_all(g, 'head', split_axis=1, concat_axis=0, tiled=True)  12.5 us
    all_to_all x1, waiting for transfers between devices, body(): dsq = lax.all_to_all(dsq, 'head', split_axis=0, concat_axis=1, tiled=True)  5.84 us
  transfers between devices with their start and end apart: 5, of which 5 were waited for; matrix products, arithmetic and copies ran while one was open for 3% of the time, Pallas kernels for 0%

profile of v1, /device:TPU:0, one launch (start us, length us, event | category | flops | bytes accessed | tf_op | source)
XLA Modules:
  0.0 229.2 jit_solution(10041747198623984834)
XLA Ops:
  7.2 0.0 all-gather.5.cloned.1.call-start
  7.2 0.7 fusion.4
  8.0 0.1 copy.34
  8.1 0.1 copy.35
  8.2 1.5 constant_dynamic-slice_fusion
  9.6 0.7 copy.42
  10.4 0.7 copy.43
  11.1 2.5 %copy.41 = bf16[256,2,8,128]{3,0,2,1:T(8,128)(2,1)} copy(bf16[256,2,8,128]{3,2,1,0:T(8,128)(2,1)} %param.5) | data formatting | bytes 2097152 | tf_op args[0]
  13.6 0.7 pad_maximum_fusion.proj_ref
  14.3 7.1 %shard_map.76 = (bf16[2,8,32,256]{3,2,1,0:T(8,128)(2,1)}, bf16[4,544,128]{2,1,0:T(8,128)(2,1)}) custom-call(bf16[2,8,256,128]{3,2,1,0:T(8,128)(2,1)} %bitcast.35, bf16[4,256,128]{2,1,0:T(8,128)(2,1)} %bitcast.44, bf16[4,256,128]{2,1,0:T(8,128)(2,1)} %bitcast.41, bf16[128,64]{1,0:T(8,128)(2,1)} %pad_maximum_fusion.proj_ref), custom_call_target="tpu_custom_call" | custom-call | tf_op jit(solution)/shard_map/pallas_call | solution.py:220
  21.4 0.0 all-gather.5.cloned.1.call-update
  21.5 1.7 copy.24
  23.1 4.2 %all-to-all-start = ((bf16[2,8,32,256]{3,2,0,1:T(8,128)(2,1)}), bf16[2,8,32,256]{3,2,0,1:T(8,128)(2,1)S(1)}, u32[]{:S(2)}, u32[]{:S(2)}) async-start(bf16[2,8,32,256]{3,2,0,1:T(8,128)(2,1)} %copy.24), calls=%async_computation | async-start | bytes 524288 | tf_op jit(solution)/shard_map/all_to_all | solution.py:248
  27.4 3.0 %copy.40 = bf16[256,2,8,128]{3,1,0,2:T(2,128)(2,1)} copy(bf16[256,2,8,128]{3,2,1,0:T(8,128)(2,1)} %param.8) | data formatting | bytes 2097152 | tf_op args[3]
  30.4 2.9 %all-to-all-done = bf16[2,8,32,256]{3,2,0,1:T(8,128)(2,1)S(1)} async-done(((bf16[2,8,32,256]{3,2,0,1:T(8,128)(2,1)}), bf16[2,8,32,256]{3,2,0,1:T(8,128)(2,1)S(1)}, u32[]{:S(2)}, u32[]{:S(2)}) %all-to-all-start) | async-done | bytes 262176 | tf_op jit(solution)/shard_map/all_to_all | solution.py:248
  33.3 3.6 %all-to-all-start.1 = ((bf16[2,8,256,128]{3,0,2,1:T(2,128)(2,1)}), bf16[2,8,256,128]{3,0,2,1:T(2,128)(2,1)S(1)}, u32[]{:S(2)}, u32[]{:S(2)}) async-start(bf16[2,8,256,128]{3,0,2,1:T(2,128)(2,1)} %bitcast.31), calls=%async_computation.1 | async-start | bytes 2097152 | tf_op jit(solution)/shard_map/all_to_all | solution.py:249
  36.8 0.0 all-gather.7.cloned.1.call-start
  36.9 0.8 copy.25
  37.7 12.5 %all-to-all-done.1 = bf16[2,8,256,128]{3,0,2,1:T(2,128)(2,1)S(1)} async-done(((bf16[2,8,256,128]{3,0,2,1:T(2,128)(2,1)}), bf16[2,8,256,128]{3,0,2,1:T(2,128)(2,1)S(1)}, u32[]{:S(2)}, u32[]{:S(2)}) %all-to-all-start.1) | async-done | bytes 1048608 | tf_op jit(solution)/shard_map/all_to_all | solution.py:249
  50.1 1.2 copy.27
  51.3 51.2 %all-gather.5.cloned.1.call-done = bf16[64,544,128]{2,1,0:T(8,128)(2,1)} async-done(((bf16[4,544,128]{2,1,0:T(8,128)(2,1)}), bf16[64,544,128]{2,1,0:T(8,128)(2,1)}) %all-gather.5.cloned.1.call-update) | async-done | bytes 8912912 | tf_op jit(solution)/shard_map/all_gather | solution.py:255
  102.5 6.4 %fusion.1.state_ref = f32[4,544,128]{2,1,0:T(8,128)} fusion(bf16[16,4,544,128]{3,2,1,0:T(8,128)(2,1)} %bitcast.37, pred[16]{0:T(512)(128)(4,1)S(1)} %iota_compare_fusion.1), kind=kLoop, calls=%fused_computation.3 | loop fusion | flops 13090816 | bytes 10027024 | tf_op jit(solution)/shard_map/reduce_sum | solution.py:256
  108.9 11.3 %shard_map.77 = (bf16[4,4,32,256]{3,2,1,0:T(8,128)(2,1)}, f32[4,256,32]{2,1,0:T(8,128)}, f32[4,256,128]{2,1,0:T(8,128)}, bf16[4,544,128]{2,1,0:T(8,128)(2,1)}) custom-call(bf16[4,4,32,256]{3,2,1,0:T(8,128)(2,1)} %bitcast.47, bf16[4,256,128]{2,1,0:T(8,128)(2,1)} %bitcast.45, bf16[4,256,128]{2,1,0:T(8,128)(2,1)} %bitcast.42, ...), custom_call_target="tpu_custom_call" | custom-call | tf_op jit(solution)/shard_map/pallas_call | solution.py:220
  120.3 0.0 all-gather.7.cloned.1.call-update
  120.3 3.5 %all-to-all-start.2 = ((bf16[4,4,32,256]{3,2,1,0:T(8,128)(2,1)}), bf16[4,4,32,256]{3,2,1,0:T(8,128)(2,1)S(1)}, u32[]{:S(2)}, u32[]{:S(2)}) async-start(bf16[4,4,32,256]{3,2,1,0:T(8,128)(2,1)} %get-tuple-element.14), calls=%async_computation.2 | async-start | bytes 524288 | tf_op jit(solution)/shard_map/all_to_all | solution.py:286
  123.8 5.8 %all-to-all-done.2 = bf16[4,4,32,256]{3,2,1,0:T(8,128)(2,1)S(1)} async-done(((bf16[4,4,32,256]{3,2,1,0:T(8,128)(2,1)}), bf16[4,4,32,256]{3,2,1,0:T(8,128)(2,1)S(1)}, u32[]{:S(2)}, u32[]{:S(2)}) %all-to-all-start.2) | async-done | bytes 262176 | tf_op jit(solution)/shard_map/all_to_all | solution.py:286
  129.6 0.7 copy.28
  130.3 66.4 %all-gather.7.cloned.1.call-done = bf16[64,544,128]{2,1,0:T(8,128)(2,1)} async-done(((bf16[4,544,128]{2,1,0:T(8,128)(2,1)}), bf16[64,544,128]{2,1,0:T(8,128)(2,1)}) %all-gather.7.cloned.1.call-update) | async-done | bytes 8912912 | tf_op jit(solution)/shard_map/all_gather | solution.py:255
  196.8 6.5 %fusion.state_ref = f32[4,544,128]{2,1,0:T(8,128)} fusion(bf16[16,4,544,128]{3,2,1,0:T(8,128)(2,1)} %bitcast.38, pred[16]{0:T(512)(128)(4,1)S(1)} %iota_compare_fusion), kind=kLoop, calls=%fused_computation.1 | loop fusion | flops 13090816 | bytes 10027024 | tf_op jit(solution)/shard_map/reduce_sum | solution.py:256
  203.3 12.5 %shard_map.78 = (bf16[2,8,256,128]{3,2,1,0:T(8,128)(2,1)}, bf16[4,256,128]{2,1,0:T(8,128)(2,1)}, bf16[4,256,128]{2,1,0:T(8,128)(2,1)}) custom-call(bf16[2,8,256,128]{3,2,1,0:T(8,128)(2,1)} %bitcast.36, bf16[2,8,32,256]{3,2,1,0:T(8,128)(2,1)} %bitcast.51, bf16[4,256,128]{2,1,0:T(8,128)(2,1)} %bitcast.46, bf16[4,256,128]{2,1,0:T(8,128)(2,1)} %bitcast.43, ...), custom_call_target="tpu_custom_call" | custom-call | tf_op jit(solution)/shard_map/pallas_call | solution.py:220
  215.8 2.9 %copy.29 = bf16[256,2,8,128]{3,2,1,0:T(8,128)(2,1)} copy(bf16[256,2,8,128]{3,0,2,1:T(8,128)(2,1)} %bitcast.48) | data formatting | bytes 2097152
  218.6 1.9 copy.30
  220.5 1.9 copy.31
  (3 shorter events, 0.0 us)
Async XLA Ops:
  7.2 95.3 %all-gather.5.cloned.1.call-start = ((), (), s32[]{:S(2)}) async-start(), calls=%async_computation.3 | async-start | bytes 9469952 | tf_op jit(solution)/shard_map/all_gather | solution.py:255
  23.1 10.1 %all-to-all-start = ((bf16[2,8,32,256]{3,2,0,1:T(8,128)(2,1)}), bf16[2,8,32,256]{3,2,0,1:T(8,128)(2,1)S(1)}, u32[]{:S(2)}, u32[]{:S(2)}) async-start(bf16[2,8,32,256]{3,2,0,1:T(8,128)(2,1)} %copy.24), calls=%async_computation | async-start | bytes 524288 | tf_op jit(solution)/shard_map/all_to_all | solution.py:248
  33.3 16.9 %all-to-all-start.1 = ((bf16[2,8,256,128]{3,0,2,1:T(2,128)(2,1)}), bf16[2,8,256,128]{3,0,2,1:T(2,128)(2,1)S(1)}, u32[]{:S(2)}, u32[]{:S(2)}) async-start(bf16[2,8,256,128]{3,0,2,1:T(2,128)(2,1)} %bitcast.31), calls=%async_computation.1 | async-start | bytes 2097152 | tf_op jit(solution)/shard_map/all_to_all | solution.py:249
  36.8 159.9 %all-gather.7.cloned.1.call-start = ((), (), s32[]{:S(2)}) async-start(), calls=%async_computation.4 | async-start | bytes 9469952 | tf_op jit(solution)/shard_map/all_gather | solution.py:255
  120.3 9.3 %all-to-all-start.2 = ((bf16[4,4,32,256]{3,2,1,0:T(8,128)(2,1)}), bf16[4,4,32,256]{3,2,1,0:T(8,128)(2,1)S(1)}, u32[]{:S(2)}, u32[]{:S(2)}) async-start(bf16[4,4,32,256]{3,2,1,0:T(8,128)(2,1)} %get-tuple-element.14), calls=%async_computation.2 | async-start | bytes 524288 | tf_op jit(solution)/shard_map/all_to_all | solution.py:286
Sparse Core Ops, SparseCore 0:
  21.6 80.8 all-gather.4
  120.4 76.3 all-gather.6

commit v2 on v1

--- a/solution.py
+++ b/solution.py
@@ -1,3 +1,5 @@
+import functools
+
 import jax
 import jax.numpy as jnp
 from jax import lax
@@ -107,7 +109,7 @@
     @pl.loop(0, k_ref.shape[0])
     def _(h):
         one, two = sketches(k_ref[h], proj, width)
-        feat = pair_features((one * two).astype(bf16).astype(f32))
+        feat = pair_features(one * two)
         v = v_ref[h]
         wide = nn(feat, ones_beside(v))
         state_ref[h] = state_with_totals(wide, v.shape[1]).astype(bf16)
@@ -117,7 +119,7 @@
         @pl.loop(0, q_ref.shape[1])
         def _(h):
             one, two = sketches(q_ref[m, h], proj, width)
-            s_ref[m, h] = (one * two).astype(bf16)
+            s_ref[m, h] = jnp.concatenate(split(one * two), axis=0)
 
 
 def main_kernel(
@@ -129,17 +131,21 @@
     members = sq_ref.shape[0]
     tokens, lanes = v_ref.shape[1:]
     one, two = sketches(k_ref[0], proj, width)
-    skt = (one * two).astype(bf16)
-    sk = (one * two).T.astype(bf16)
+    skt = jnp.concatenate(split(one * two), axis=0)
+    sk_high, sk_low = split((one * two).T)
     v = v_ref[0]
     sqt = jnp.concatenate([sq_ref[m, 0] for m in range(members)], axis=1)
-    sq = sqt.astype(f32)
+    sq = sqt[:width].astype(f32) + sqt[width:].astype(f32)
     gout = jnp.concatenate([g_ref[m, 0].astype(f32).T for m in range(members)], axis=1)
     feat = pair_features(sq)
-    state = state_ref[0][:pairs]
-    totals = unpack_totals(state_ref[0][pairs:], pairs)
-
-    inside = nn(sk, sqt)
+    held = state_ref[0].astype(f32)
+    state = held[:pairs]
+    totals = unpack_totals(held[pairs:], pairs)
+
+    inside = nn(
+        jnp.concatenate([sk_high, sk_high, sk_low], axis=1),
+        jnp.concatenate([sqt, sqt[:width]], axis=0),
+    )
     row = lax.broadcasted_iota(jnp.int32, inside.shape, 0)
     column = lax.rem(lax.broadcasted_iota(jnp.int32, inside.shape, 1), tokens)
     inside = jnp.where(row <= column, inside, 0.0)
@@ -158,7 +164,8 @@
     low = rows.astype(bf16)
     dscores = nn(v, low) + correction
     edge = (dscores * inside * (2.0 / width**2)).astype(bf16)
-    dsk_ref[0] = nt(edge, sqt)
+    dsk_both = nt(edge, sqt)
+    dsk_ref[0] = dsk_both[:, :width] + dsk_both[:, width:]
     dv_ref[0] = nt(weights, low)
 
     corr_high = correction.astype(bf16).astype(f32)
@@ -170,7 +177,8 @@
         [totals, totals, jnp.zeros((lanes - 2, pairs), f32)], axis=0
     ).T
     cotangent = nn(jnp.concatenate([state, total_columns], axis=1).astype(bf16), spread)
-    dsq = nn(skt, edge) + pair_back(cotangent, sq)
+    dsq_both = nn(skt, edge)
+    dsq = dsq_both[:width] + dsq_both[width:] + pair_back(cotangent, sq)
     for m in range(members):
         dsq_ref[m, 0] = dsq[:, m * tokens : (m + 1) * tokens].astype(bf16)
 
@@ -192,12 +200,13 @@
     @pl.loop(0, k_ref.shape[0])
     def _(h):
         one, two = sketches(k_ref[h], proj, width)
-        s = (one * two).astype(bf16).astype(f32)
+        s = one * two
         feat = pair_features(s)
         v = v_ref[h]
         lanes = v.shape[1]
-        state = state_ref[h][:pairs]
-        totals = unpack_totals(state_ref[h][pairs:], pairs)
+        held = state_ref[h].astype(f32)
+        state = held[:pairs]
+        totals = unpack_totals(held[pairs:], pairs)
         total_columns = jnp.concatenate([totals, jnp.zeros((lanes - 1, pairs), f32)], axis=0).T
         cotangent = nt(
             jnp.concatenate([state, total_columns], axis=1).astype(bf16), ones_beside(v)
@@ -223,6 +232,228 @@
         compiler_params=pltpu.CompilerParams(vmem_limit_bytes=GRANT),
         **more,
     )(*args)
+
+
+TEAM = 4
+
+
+def scan_kernel(reverse, swaps, spread, *refs):
+    part = refs[0]
+    sources = refs[1 : 1 + swaps]
+    out = refs[1 + swaps]
+    targets = refs[2 + swaps : 2 + 2 * swaps]
+    (near, far, total, result, send1, recv1, send2, recv2, send3, recv3) = refs[
+        2 + 2 * swaps : 12 + 2 * swaps
+    ]
+    send_y, recv_y, local = refs[12 + 2 * swaps :]
+    blocks = lax.axis_size("ctx")
+    sides = lax.axis_size("head")
+    groups = blocks // TEAM
+    place = lax.axis_index("ctx")
+    side = lax.axis_index("head")
+    rank = lax.rem(place, TEAM)
+    group = place // TEAM
+    step = -1 if reverse else 1
+    chunks = part.shape[1]
+
+    barrier = pltpu.get_barrier_semaphore()
+
+    def greet(target):
+        pl.semaphore_signal(
+            barrier, inc=1, device_id=target, device_id_type=pl.DeviceIdType.MESH
+        )
+
+    for k in range(1, TEAM):
+        greet({"ctx": group * TEAM + lax.rem(rank + k, TEAM)})
+    for k in range(1, groups):
+        greet({"ctx": lax.rem(group + k, groups) * TEAM + rank})
+    for k in range(1, sides):
+        greet({"head": lax.rem(side + k, sides)})
+    pl.semaphore_wait(barrier, TEAM - 1 + groups - 1 + sides - 1)
+
+    def remote(source, target, send, recv, device):
+        return pltpu.make_async_remote_copy(
+            src_ref=source,
+            dst_ref=target,
+            send_sem=send,
+            recv_sem=recv,
+            device_id=device,
+            device_id_type=pl.DeviceIdType.MESH,
+        )
+
+    def member(p):
+        return {"ctx": group * TEAM + p}
+
+    def collect(p, c, slot):
+        return remote(
+            part.at[p, c], near.at[slot, c], send1.at[p, c], recv1.at[slot, c], member(p)
+        )
+
+    def across(k, c):
+        return remote(
+            total.at[c],
+            far.at[k - 1, c],
+            send2.at[k - 1, c],
+            recv2.at[k - 1, c],
+            {"ctx": (group + step * k) * TEAM + rank},
+        )
+
+    def hand(p, c, slot):
+        return remote(
+            result.at[p, c], out.at[slot, c], send3.at[p, c], recv3.at[slot, c], member(p)
+        )
+
+    def ahead(k):
+        return group - k >= 0 if reverse else group + k < groups
+
+    def behind(k):
+        return group + k < groups if reverse else group - k >= 0
+
+    def swap(n, k):
+        source, target = sources[n], targets[n]
+        to = lax.rem(side + k, sides)
+        return remote(
+            view(source, to), view_to(target, side), send_y.at[n, k - 1], recv_y.at[n, k - 1],
+            {"head": to},
+        )
+
+    def view(source, to):
+        if spread:
+            count = source.shape[1] // sides
+            return source.at[:, pl.ds(to * count, count)]
+        count = source.shape[0] // sides
+        return source.at[pl.ds(to * count, count)]
+
+    def view_to(target, at):
+        if spread:
+            count = target.shape[0] // sides
+            return target.at[pl.ds(at * count, count)]
+        count = target.shape[1] // sides
+        return target.at[:, pl.ds(at * count, count)]
+
+    def keep(n):
+        return pltpu.make_async_copy(view(sources[n], side), view_to(targets[n], side), local.at[n])
+
+    for c in range(chunks):
+        for p in range(TEAM):
+
+            @pl.when(p != rank)
+            def _():
+                collect(p, c, rank).start()
+
+    for n in range(swaps):
+        for k in range(1, sides):
+            swap(n, k).start()
+        keep(n).start()
+
+    for c in range(chunks):
+        near[rank, c] = part[rank, c]
+        for p in range(TEAM):
+
+            @pl.when(p != rank)
+            def _():
+                collect(p, c, p).wait_recv()
+
+        total[c] = sum(near[p, c].astype(f32) for p in range(TEAM)).astype(bf16)
+        for k in range(1, groups):
+
+            @pl.when(ahead(k))
+            def _():
+                across(k, c).start()
+
+    zeros = jnp.zeros(part.shape[2:], f32)
+    for c in range(chunks):
+        running = zeros
+        for k in range(1, groups):
+
+            @pl.when(behind(k))
+            def _():
+                across(k, c).wait_recv()
+
+            @pl.when(jnp.logical_not(behind(k)))
+            def _():
+                far[k - 1, c] = zeros.astype(bf16)
+
+            running = running + far[k - 1, c].astype(f32)
+        for p in reversed(range(TEAM)) if reverse else range(TEAM):
+            result[p, c] = running.astype(bf16)
+            running = running + near[p, c].astype(f32)
+
+            @pl.when(p != rank)
+            def _():
+                hand(p, c, rank).start()
+
+        out[rank, c] = result[rank, c]
+
+    for c in range(chunks):
+        for p in range(TEAM):
+
+            @pl.when(p != rank)
+            def _():
+                hand(p, c, p).wait_recv()
+
+    for n in range(swaps):
+        for k in range(1, sides):
+            swap(n, k).wait_recv()
+            swap(n, k).wait_send()
+        keep(n).wait()
+    for c in range(chunks):
+        for p in range(TEAM):
+
+            @pl.when(p != rank)
+            def _():
+                collect(p, c, rank).wait_send()
+                hand(p, c, rank).wait_send()
+
+        for k in range(1, groups):
+
+            @pl.when(ahead(k))
+            def _():
+                across(k, c).wait_send()
+
+
+def scan(part, others, reverse, spread, number):
+    heads, rows, lanes = part.shape
+    piece = heads * rows // TEAM
+    chunks = 2 if piece % 32 == 0 else 1
+    shape = (TEAM, chunks, piece // chunks, lanes)
+    sides = lax.axis_size("head")
+    groups = lax.axis_size("ctx") // TEAM
+    swaps = len(others)
+    whole = pl.BlockSpec(memory_space=pltpu.VMEM)
+    apart = pl.BlockSpec(memory_space=pl.ANY)
+    sems = pltpu.SemaphoreType.DMA
+
+    def moved(a):
+        one, two = a.shape[:2]
+        lead = (one * sides, two // sides) if spread else (one // sides, two * sides)
+        return jax.ShapeDtypeStruct(lead + a.shape[2:], a.dtype)
+
+    results = pl.pallas_call(
+        functools.partial(scan_kernel, reverse, swaps, spread),
+        out_shape=(jax.ShapeDtypeStruct(shape, bf16),) + tuple(moved(a) for a in others),
+        in_specs=[whole] + [apart] * swaps,
+        out_specs=(whole,) + (apart,) * swaps,
+        scratch_shapes=[
+            pltpu.VMEM(shape, bf16),
+            pltpu.VMEM((max(groups - 1, 1),) + shape[1:], bf16),
+            pltpu.VMEM(shape[1:], bf16),
+            pltpu.VMEM(shape, bf16),
+            sems((TEAM, chunks)),
+            sems((TEAM, chunks)),
+            sems((max(groups - 1, 1), chunks)),
+            sems((max(groups - 1, 1), chunks)),
+            sems((TEAM, chunks)),
+            sems((TEAM, chunks)),
+            sems((swaps, max(sides - 1, 1))),
+            sems((swaps, max(sides - 1, 1))),
+            sems((swaps,)),
+        ],
+        compiler_params=pltpu.CompilerParams(
+            collective_id=number, has_side_effects=True, vmem_limit_bytes=GRANT
+        ),
+    )(part.reshape(shape), *others)
+    return (results[0].reshape(part.shape),) + tuple(results[1:])
 
 
 def body(queries, keys, values, dout, signs):
@@ -242,20 +473,10 @@
     shape = jax.ShapeDtypeStruct
     sq, block_state = call(
         first_kernel,
-        (shape((mine, heads_all, width, tokens), bf16), shape((owned, rows, hd), bf16)),
+        (shape((mine, heads_all, 2 * width, tokens), bf16), shape((owned, rows, hd), bf16)),
         (q, k, v, proj),
     )
-    sq = lax.all_to_all(sq, "head", split_axis=1, concat_axis=0, tiled=True)
-    g = lax.all_to_all(g, "head", split_axis=1, concat_axis=0, tiled=True)
-    count = lax.axis_size("ctx")
-    place = lax.axis_index("ctx")
-    source = lax.broadcasted_iota(jnp.int32, (count, 1, 1, 1), 0)
-
-    def scan(part, keep):
-        gathered = lax.all_gather(part, "ctx")
-        return jnp.sum(jnp.where(keep, gathered.astype(f32), 0.0), 0)
-
-    state = scan(block_state, source < place)
+    state, sq, g = scan(block_state, (sq, g), False, True, 0)
     by_member = lambda h: (0, h, 0, 0)
     by_head = lambda h: (h, 0, 0)
     dsq, dsk, dv, part = call(
@@ -269,7 +490,7 @@
         (sq, k, v, g, proj, state),
         grid=(owned,),
         in_specs=[
-            pl.BlockSpec((members, 1, width, tokens), by_member),
+            pl.BlockSpec((members, 1, 2 * width, tokens), by_member),
             pl.BlockSpec((1, tokens, hd), by_head),
             pl.BlockSpec((1, tokens, hd), by_head),
             pl.BlockSpec((members, 1, tokens, hd), by_member),
@@ -283,8 +504,7 @@
             pl.BlockSpec((1, rows, hd), by_head),
         ),
     )
-    dsq = lax.all_to_all(dsq, "head", split_axis=0, concat_axis=1, tiled=True)
-    later = scan(part, source > place)
+    later, dsq = scan(part, (dsq,), True, False, 1)
     dq, dk, dv = call(
         last_kernel,
         (

time: 230 us -> 105 us (0.46)
  waiting for transfers between devices: 139 us -> 0 us
  Pallas kernels: 31 us -> 91.7 us
  between operations: 14.1 us -> 0.68 us
  other arithmetic: 13.6 us -> 0.72 us
  starting transfers between devices: 11.3 us -> 0 us
  local copies, waits for them, and re-layouts: 20.3 us -> 11.2 us
    all_gather x2 -> x0, waiting for transfers between devices: 118 us -> none  [scan(): gathered = lax.all_gather(part, 'ctx')]
    pallas_call x0 -> x2, Pallas kernels: none -> 59.9 us  [scan(): pl.pallas_call(functools.partial(scan_kernel, reverse, swaps, spread), ou...]
    all_to_all x3 -> x0, waiting for transfers between devices: 21.2 us -> none  [the longest x1 12.5 us: body(): g = lax.all_to_all(g, 'head', split_axis=1, concat_axis=0, tiled=True)]
    reduce_sum x2 -> x0, other arithmetic: 12.9 us -> none  [scan(): return jnp.sum(jnp.where(keep, gathered.astype(f32), 0.0), 0)]
    all_to_all x3 -> x0, starting transfers between devices: 11.3 us -> none  [the longest x1 4.23 us: body(): sq = lax.all_to_all(sq, 'head', split_axis=1, concat_axis=0, tiled=True)]
    unnamed x9 -> x19, local copies, waits for them, and re-layouts: 13.7 us -> 9 us
    all_to_all x3 -> x0, local copies, waits for them, and re-layouts: 2.67 us -> none  [the longest x1 1.17 us: body(): g = lax.all_to_all(g, 'head', split_axis=1, concat_axis=0, tiled=True)]
  transfers between devices with their start and end apart: 5 -> 0, of which waited for: 5 -> 0; matrix products, arithmetic and copies ran while one was open for 3% -> 0% of each run, Pallas kernels for 0% -> 0%
where the time goes in v2:
time: 105 us; the launch traced here: 104 us
  Pallas kernels  91.7 us (87%)
  local copies, waits for them, and re-layouts  11.2 us (11%)
    pallas_call x2, Pallas kernels, scan(): pl.pallas_call(functools.partial(scan_kernel, reverse, swaps, spread), ou...  59.9 us
    pallas_call x3, Pallas kernels, call(): pl.pallas_call(kernel, out_shape=outs, compiler_params=pltpu.CompilerPara...  31.7 us
    unnamed x19, local copies, waits for them, and re-layouts  9 us

profile of v2, /device:TPU:0, one launch (start us, length us, event | category | flops | bytes accessed | tf_op | source)
XLA Modules:
  0.0 104.3 jit_solution(11790163201342246917)
XLA Ops:
  0.6 0.0 copy-start.4
  0.6 0.8 fusion.2
  1.4 0.1 copy.19
  1.5 0.1 copy.20
  1.7 0.7 pad_maximum_fusion.proj_ref
  2.4 0.0 copy-done.4
  2.4 0.0 copy-start
  2.4 1.4 %constant_dynamic-slice_fusion = (bf16[256,4,128]{2,1,0:T(4,128)(2,1)S(1)}, bf16[256,4,128]{2,1,0:T(4,128)(2,1)S(1)}) fusion(bf16[256,8,128]{2,1,0:T(8,128)(2,1)S(1)} %copy-done.4, s32[]{:T(128)S(6)} %select_n.4, bf16[256,8,128]{2,1,0:T(8,128)(2,1)} %param.6), kind=kLoop, calls=%fused_computation.9 | loop fusion | bytes 1048580 | tf_op jit(solution)/shard_map/dynamic_slice | solution.py:468
  3.8 0.7 copy.27
  4.5 0.7 copy.28
  5.3 0.0 copy-done
  5.3 0.0 copy-start.1
  5.3 1.2 %copy.26 = bf16[256,2,8,128]{3,0,2,1:T(8,128)(2,1)} copy(bf16[256,2,8,128]{3,2,1,0:T(8,128)(2,1)S(1)} %copy-done) | data formatting | bytes 2097152 | tf_op args[0]
  6.5 0.1 copy-done.1
  6.6 1.3 %copy.25 = bf16[256,2,8,128]{3,0,2,1:T(8,128)(2,1)} copy(bf16[256,2,8,128]{3,2,1,0:T(8,128)(2,1)S(1)} %copy-done.1) | data formatting | bytes 2097152 | tf_op args[3]
  7.8 7.3 %shard_map.76 = (bf16[2,8,64,256]{3,2,1,0:T(8,128)(2,1)}, bf16[4,544,128]{2,1,0:T(8,128)(2,1)}) custom-call(bf16[2,8,256,128]{3,2,1,0:T(8,128)(2,1)} %bitcast.23, bf16[4,256,128]{2,1,0:T(8,128)(2,1)} %bitcast.29, bf16[4,256,128]{2,1,0:T(8,128)(2,1)} %bitcast.26, bf16[128,64]{1,0:T(8,128)(2,1)} %pad_maximum_fusion.proj_ref), custom_call_target="tpu_custom_call" | custom-call | tf_op jit(solution)/shard_map/pallas_call | solution.py:229
  15.1 32.3 %shard_map.77 = (bf16[4,2,272,128]{3,2,1,0:T(8,128)(2,1)}, bf16[4,4,64,256]{3,2,1,0:T(8,128)(2,1)}, bf16[4,4,256,128]{3,2,1,0:T(8,128)(2,1)}) custom-call(bf16[4,2,272,128]{3,2,1,0:T(8,128)(2,1)} %bitcast.36, bf16[2,8,64,256]{3,2,1,0:T(8,128)(2,1)} %get-tuple-element.18.refs_1_, bf16[2,8,256,128]{3,2,1,0:T(8,128)(2,1)} %bitcast.25), custom_call_target="tpu_custom_call" | custom-call | tf_op jit(solution)/shard_map/pallas_call | solution.py:432
  47.4 12.1 %shard_map.78 = (bf16[4,4,32,256]{3,2,1,0:T(8,128)(2,1)}, f32[4,256,32]{2,1,0:T(8,128)}, f32[4,256,128]{2,1,0:T(8,128)}, bf16[4,544,128]{2,1,0:T(8,128)(2,1)}) custom-call(bf16[4,4,64,256]{3,2,1,0:T(8,128)(2,1)} %get-tuple-element.19.sq_ref, bf16[4,256,128]{2,1,0:T(8,128)(2,1)} %bitcast.30, bf16[4,256,128]{2,1,0:T(8,128)(2,1)} %bitcast.27, ...), custom_call_target="tpu_custom_call" | custom-call | tf_op jit(solution)/shard_map/pallas_call | solution.py:229
  59.6 27.6 %shard_map.79 = (bf16[4,2,272,128]{3,2,1,0:T(8,128)(2,1)}, bf16[2,8,32,256]{3,2,1,0:T(8,128)(2,1)}) custom-call(bf16[4,2,272,128]{3,2,1,0:T(8,128)(2,1)} %bitcast.35, bf16[4,4,32,256]{3,2,1,0:T(8,128)(2,1)} %get-tuple-element.23.refs_1_), custom_call_target="tpu_custom_call" | custom-call | tf_op jit(solution)/shard_map/pallas_call | solution.py:432
  87.1 12.3 %shard_map.80 = (bf16[2,8,256,128]{3,2,1,0:T(8,128)(2,1)}, bf16[4,256,128]{2,1,0:T(8,128)(2,1)}, bf16[4,256,128]{2,1,0:T(8,128)(2,1)}) custom-call(bf16[2,8,256,128]{3,2,1,0:T(8,128)(2,1)} %bitcast.24, bf16[2,8,32,256]{3,2,1,0:T(8,128)(2,1)} %get-tuple-element.24.ds_ref, bf16[4,256,128]{2,1,0:T(8,128)(2,1)} %bitcast.31, bf16[4,256,128]{2,1,0:T(8,128)(2,1)} %bitcast.28, ...), custom_call_target="tpu_custom_call" | custom-call | tf_op jit(solution)/shard_map/pallas_call | solution.py:229
  99.5 0.0 copy-start.3
  99.5 2.9 %copy.14 = bf16[256,2,8,128]{3,2,1,0:T(8,128)(2,1)} copy(bf16[256,2,8,128]{3,0,2,1:T(8,128)(2,1)} %bitcast.32) | data formatting | bytes 2097152
  102.4 0.0 copy-done.3
  102.4 0.0 copy-start.2
  102.4 0.9 copy.15
  103.3 0.0 copy-done.2
  103.4 0.9 copy.16
  (1 shorter events, 0.0 us)
Async XLA Ops:
  0.6 1.7 %copy-start.4 = (bf16[256,8,128]{2,1,0:T(8,128)(2,1)S(1)}, bf16[256,8,128]{2,1,0:T(8,128)(2,1)}, u32[]{:S(2)}) copy-start(bf16[256,8,128]{2,1,0:T(8,128)(2,1)} %param.7) | copy-start | bytes 1572868
  2.4 2.9 %copy-start = (bf16[256,2,8,128]{3,2,1,0:T(8,128)(2,1)S(1)}, bf16[256,2,8,128]{3,2,1,0:T(8,128)(2,1)}, u32[]{:S(2)}) copy-start(bf16[256,2,8,128]{3,2,1,0:T(8,128)(2,1)} %param.5) | copy-start | bytes 3145732
  5.3 1.3 %copy-start.1 = (bf16[256,2,8,128]{3,2,1,0:T(8,128)(2,1)S(1)}, bf16[256,2,8,128]{3,2,1,0:T(8,128)(2,1)}, u32[]{:S(2)}) copy-start(bf16[256,2,8,128]{3,2,1,0:T(8,128)(2,1)} %param.8) | copy-start | bytes 3145732
  99.5 2.9 %copy-start.3 = (bf16[4,256,128]{2,1,0:T(8,128)(2,1)S(1)}, bf16[4,256,128]{2,1,0:T(8,128)(2,1)}, u32[]{:S(2)}) copy-start(bf16[4,256,128]{2,1,0:T(8,128)(2,1)} %get-tuple-element.29) | copy-start | bytes 786436
  102.4 1.0 copy-start.2

commit v3 on v1

--- a/solution.py
+++ b/solution.py
@@ -100,26 +100,6 @@
     return jnp.concatenate([wide[:, :lanes], pack_totals(wide[:, lanes:], lanes)], axis=0)
 
 
-def first_kernel(q_ref, k_ref, v_ref, proj_ref, s_ref, state_ref):
-    proj = proj_ref[...]
-    width = proj.shape[1] // 2
-
-    @pl.loop(0, k_ref.shape[0])
-    def _(h):
-        one, two = sketches(k_ref[h], proj, width)
-        feat = pair_features((one * two).astype(bf16).astype(f32))
-        v = v_ref[h]
-        wide = nn(feat, ones_beside(v))
-        state_ref[h] = state_with_totals(wide, v.shape[1]).astype(bf16)
-
-    @pl.loop(0, q_ref.shape[0])
-    def _(m):
-        @pl.loop(0, q_ref.shape[1])
-        def _(h):
-            one, two = sketches(q_ref[m, h], proj, width)
-            s_ref[m, h] = (one * two).astype(bf16)
-
-
 def main_kernel(
     sq_ref, k_ref, v_ref, g_ref, proj_ref, state_ref, dsq_ref, dsk_ref, dv_ref, out_ref
 ):
@@ -129,17 +109,21 @@
     members = sq_ref.shape[0]
     tokens, lanes = v_ref.shape[1:]
     one, two = sketches(k_ref[0], proj, width)
-    skt = (one * two).astype(bf16)
-    sk = (one * two).T.astype(bf16)
+    skt = jnp.concatenate(split(one * two), axis=0)
+    sk_high, sk_low = split((one * two).T)
     v = v_ref[0]
     sqt = jnp.concatenate([sq_ref[m, 0] for m in range(members)], axis=1)
-    sq = sqt.astype(f32)
+    sq = sqt[:width].astype(f32) + sqt[width:].astype(f32)
     gout = jnp.concatenate([g_ref[m, 0].astype(f32).T for m in range(members)], axis=1)
     feat = pair_features(sq)
-    state = state_ref[0][:pairs]
-    totals = unpack_totals(state_ref[0][pairs:], pairs)
-
-    inside = nn(sk, sqt)
+    held = state_ref[0].astype(f32)
+    state = held[:pairs]
+    totals = unpack_totals(held[pairs:], pairs)
+
+    inside = nn(
+        jnp.concatenate([sk_high, sk_high, sk_low], axis=1),
+        jnp.concatenate([sqt, sqt[:width]], axis=0),
+    )
     row = lax.broadcasted_iota(jnp.int32, inside.shape, 0)
     column = lax.rem(lax.broadcasted_iota(jnp.int32, inside.shape, 1), tokens)
     inside = jnp.where(row <= column, inside, 0.0)
@@ -158,7 +142,8 @@
     low = rows.astype(bf16)
     dscores = nn(v, low) + correction
     edge = (dscores * inside * (2.0 / width**2)).astype(bf16)
-    dsk_ref[0] = nt(edge, sqt)
+    dsk_both = nt(edge, sqt)
+    dsk_ref[0] = dsk_both[:, :width] + dsk_both[:, width:]
     dv_ref[0] = nt(weights, low)
 
     corr_high = correction.astype(bf16).astype(f32)
@@ -170,7 +155,8 @@
         [totals, totals, jnp.zeros((lanes - 2, pairs), f32)], axis=0
     ).T
     cotangent = nn(jnp.concatenate([state, total_columns], axis=1).astype(bf16), spread)
-    dsq = nn(skt, edge) + pair_back(cotangent, sq)
+    dsq_both = nn(skt, edge)
+    dsq = dsq_both[:width] + dsq_both[width:] + pair_back(cotangent, sq)
     for m in range(members):
         dsq_ref[m, 0] = dsq[:, m * tokens : (m + 1) * tokens].astype(bf16)
 
@@ -179,41 +165,6 @@
     out_ref[0] = state_with_totals(jnp.concatenate([wide[:, :lanes], both], axis=1), lanes).astype(
         bf16
     )
-
-
-def last_kernel(
-    q_ref, ds_ref, k_ref, v_ref, proj_ref, state_ref, dsk_ref, dv_ref, dq_ref, dk_ref, dvo_ref
-):
-    proj = proj_ref[...]
-    width = proj.shape[1] // 2
-    pairs = pair_count(width)
-    inverse = k_ref.shape[-1] ** (-0.5)
-
-    @pl.loop(0, k_ref.shape[0])
-    def _(h):
-        one, two = sketches(k_ref[h], proj, width)
-        s = (one * two).astype(bf16).astype(f32)
-        feat = pair_features(s)
-        v = v_ref[h]
-        lanes = v.shape[1]
-        state = state_ref[h][:pairs]
-        totals = unpack_totals(state_ref[h][pairs:], pairs)
-        total_columns = jnp.concatenate([totals, jnp.zeros((lanes - 1, pairs), f32)], axis=0).T
-        cotangent = nt(
-            jnp.concatenate([state, total_columns], axis=1).astype(bf16), ones_beside(v)
-        )
-        ds = dsk_ref[h].T + pair_back(cotangent, s)
-        dk_ref[h] = finish(ds, one, two, proj, inverse).astype(bf16)
-        state_rows = doubled(state.T, width, 1).astype(bf16)
-        dvo_ref[h] = (dv_ref[h] + nn(state_rows, feat).T).astype(bf16)
-
-    @pl.loop(0, q_ref.shape[0])
-    def _(m):
-        @pl.loop(0, q_ref.shape[1])
-        def _(h):
-            one, two = sketches(q_ref[m, h], proj, width)
-            ds = ds_ref[m, h].astype(f32)
-            dq_ref[m, h] = finish(ds, one, two, proj, inverse).astype(bf16)
 
 
 def call(kernel, outs, args, **more):
@@ -222,6 +173,344 @@
         out_shape=outs,
         compiler_params=pltpu.CompilerParams(vmem_limit_bytes=GRANT),
         **more,
+    )(*args)
+
+
+TEAM = 4
+
+
+def run_scan(reverse, spread, part, sources, out, targets, scratch, ready, fill, early, late, final):
+    (mate, chip, other, run_in, run_out, base_out, base_in, give) = scratch[:8]
+    (mate_sems, chip_sems, run_sems, base_sems, give_sems, send_y, recv_y, local) = scratch[8:]
+    swaps = len(sources)
+    blocks = lax.axis_size("ctx")
+    sides = lax.axis_size("head")
+    groups = blocks // TEAM
+    place = lax.axis_index("ctx")
+    side = lax.axis_index("head")
+    rank = lax.rem(place, TEAM)
+    group = place // TEAM
+    x = rank // 2
+    core = lax.rem(rank, 2)
+    chunks = part.shape[1]
+    late_x = (1 - x if reverse else x).astype(f32)
+    late_core = (1 - core if reverse else core).astype(f32)
+    team = group * TEAM
+    core_peer = {"ctx": team + 2 * x + 1 - core}
+    chip_peer = {"ctx": team + 2 * (1 - x) + core}
+    next_group = group - 1 if reverse else group + 1
+    has_next = group > 0 if reverse else group < groups - 1
+    has_last = group < groups - 1 if reverse else group > 0
+
+    barrier = pltpu.get_barrier_semaphore()
+
+    def greet(target):
+        pl.semaphore_signal(
+            barrier, inc=1, device_id=target, device_id_type=pl.DeviceIdType.MESH
+        )
+
+    greet(core_peer)
+    greet(chip_peer)
+    ends = 0
+    if groups > 1:
+        ends = 2
+        greet({"ctx": lax.rem(group + 1, groups) * TEAM + rank})
+        greet({"ctx": lax.rem(group + groups - 1, groups) * TEAM + rank})
+    for k in range(1, sides):
+        greet({"head": lax.rem(side + k, sides)})
+    pl.semaphore_wait(barrier, 2 + ends + sides - 1)
+
+    def remote(source, target, send, recv, device):
+        return pltpu.make_async_remote_copy(
+            src_ref=source,
+            dst_ref=target,
+            send_sem=send,
+            recv_sem=recv,
+            device_id=device,
+            device_id_type=pl.DeviceIdType.MESH,
+        )
+
+    def to_mate(at, c):
+        return remote(
+            part.at[2 * at + 1 - core, c],
+            mate.at[at, c],
+            mate_sems.at[0, at, c],
+            mate_sems.at[1, at, c],
+            core_peer,
+        )
+
+    def to_chip(c):
+        return remote(
+            chip.at[c], other.at[c], chip_sems.at[0, c], chip_sems.at[1, c], chip_peer
+        )
+
+    def to_next(c):
+        return remote(
+            run_out.at[c],
+            run_in.at[c],
+            run_sems.at[0, c],
+            run_sems.at[1, c],
+            {"ctx": next_group * TEAM + rank},
+        )
+
+    def to_base(c):
+        return remote(
+            base_out.at[c], base_in.at[c], base_sems.at[0, c], base_sems.at[1, c], chip_peer
+        )
+
+    def to_give(at, c, to):
+        return remote(
+            give.at[at, c],
+            out.at[2 * at + to, c],
+            give_sems.at[0, at, c],
+            give_sems.at[1, at, c],
+            core_peer,
+        )
+
+    def swap(n, k):
+        source, target = sources[n], targets[n]
+        to = lax.rem(side + k, sides)
+        return remote(
+            view(source, to), view_to(target, side), send_y.at[n, k - 1], recv_y.at[n, k - 1],
+            {"head": to},
+        )
+
+    def view(source, to):
+        if spread:
+            count = source.shape[1] // sides
+            return source.at[:, pl.ds(to * count, count)]
+        count = source.shape[0] // sides
+        return source.at[pl.ds(to * count, count)]
+
+    def view_to(target, at):
+        if spread:
+            count = target.shape[0] // sides
+            return target.at[pl.ds(at * count, count)]
+        count = target.shape[1] // sides
+        return target.at[:, pl.ds(at * count, count)]
+
+    def keep(n):
+        return pltpu.make_async_copy(view(sources[n], side), view_to(targets[n], side), local.at[n])
+
+    def wide(ref, *at):
+        return ref[at].astype(f32)
+
+    def deliver(at, c, base):
+        mine, theirs = wide(part, 2 * at + core, c), wide(mate, at, c)
+        give[at, c] = (base + mine * (1.0 - late_core)).astype(bf16)
+        to_give(at, c, core).start()
+        out[2 * at + core, c] = (base + theirs * late_core).astype(bf16)
+
+    def begin(n):
+        for k in range(1, sides):
+            swap(n, k).start()
+        keep(n).start()
+
+    def end(n):
+        for k in range(1, sides):
+            swap(n, k).wait()
+        keep(n).wait()
+
+    for n in range(ready):
+        begin(n)
+    fill()
+    for c in range(chunks):
+        to_mate(1 - x, c).start()
+        to_mate(x, c).start()
+
+    for c in range(chunks):
+        to_mate(1 - x, c).wait_recv()
+        chip[c] = (wide(part, 2 * (1 - x) + core, c) + wide(mate, 1 - x, c)).astype(bf16)
+        to_chip(c).start()
+
+    early()
+    for n in range(ready, swaps):
+        begin(n)
+
+    @pl.when(has_last)
+    def _():
+        late(end)
+
+    for c in range(chunks):
+        to_mate(x, c).wait_recv()
+        to_chip(c).wait_recv()
+        here = wide(part, rank, c) + wide(mate, x, c)
+        there = wide(other, c)
+
+        @pl.when(has_last)
+        def _():
+            to_next(c).wait_recv()
+
+        @pl.when(jnp.logical_not(has_last))
+        def _():
+            run_in[c] = jnp.zeros_like(run_in[c])
+
+        before = wide(run_in, c)
+        run_out[c] = (before + here + there).astype(bf16)
+
+        @pl.when(has_next)
+        def _():
+            to_next(c).start()
+
+        base_out[c] = (before + here * (1.0 - late_x)).astype(bf16)
+        to_base(c).start()
+        deliver(x, c, before + there * late_x)
+
+    @pl.when(jnp.logical_not(has_last))
+    def _():
+        late(end)
+
+    for c in range(chunks):
+        to_base(c).wait_recv()
+        deliver(1 - x, c, wide(base_in, c))
+
+    final(end)
+    for c in range(chunks):
+        for at in (x, 1 - x):
+            to_give(at, c, 1 - core).wait_recv()
+            to_give(at, c, core).wait_send()
+            to_mate(at, c).wait_send()
+        to_chip(c).wait_send()
+        to_base(c).wait_send()
+
+        @pl.when(has_next)
+        def _():
+            to_next(c).wait_send()
+
+
+def piece_of(buffer, h, j, per):
+    at = h * per + j
+    return at // buffer.shape[1], lax.rem(at, buffer.shape[1])
+
+
+def first_kernel(q_ref, k_ref, v_ref, g_ref, proj_ref, out, s_out, g_out, part, s_held, *scratch):
+    proj = proj_ref[...]
+    width = proj.shape[1] // 2
+    owned = k_ref.shape[0]
+    per = part.shape[0] * part.shape[1] // owned
+    rows = part.shape[2]
+
+    def fill():
+        @pl.loop(0, owned)
+        def _(h):
+            one, two = sketches(k_ref[h], proj, width)
+            v = v_ref[h]
+            wide = nn(pair_features(one * two), ones_beside(v))
+            state = state_with_totals(wide, v.shape[1]).astype(bf16)
+            for j in range(per):
+                part[piece_of(part, h, j, per)] = state[j * rows : (j + 1) * rows]
+
+    def early():
+        @pl.loop(0, q_ref.shape[0])
+        def _(m):
+            @pl.loop(0, q_ref.shape[1])
+            def _(h):
+                one, two = sketches(q_ref[m, h], proj, width)
+                s_held[m, h] = jnp.concatenate(split(one * two), axis=0)
+
+    run_scan(
+        False, True, part, (g_ref, s_held), out, (g_out, s_out), scratch, 1, fill, early,
+        lambda end: None,
+        lambda end: (end(0), end(1)),
+    )
+
+
+def last_kernel(
+    part, q_ref, ds_ref, k_ref, v_ref, proj_ref, dsk_ref, dv_ref, dq_ref, dk_ref, dvo_ref,
+    state_ref, ds_all, *scratch,
+):
+    proj = proj_ref[...]
+    width = proj.shape[1] // 2
+    pairs = pair_count(width)
+    owned = k_ref.shape[0]
+    per = part.shape[0] * part.shape[1] // owned
+    inverse = k_ref.shape[-1] ** (-0.5)
+    side = lax.axis_index("head")
+    mine, heads = q_ref.shape[:2]
+
+    def query_gradient(m, h, ds):
+        one, two = sketches(q_ref[m, h], proj, width)
+        dq_ref[m, h] = finish(ds.astype(f32), one, two, proj, inverse).astype(bf16)
+
+    def early():
+        @pl.loop(0, mine)
+        def _(m):
+            @pl.loop(0, owned)
+            def _(h):
+                query_gradient(m, side * owned + h, ds_ref[side * mine + m, h])
+
+    def late(end):
+        end(0)
+
+        @pl.loop(0, mine)
+        def _(m):
+            @pl.loop(owned, heads)
+            def _(k):
+                h = lax.rem(side * owned + k, heads)
+                query_gradient(m, h, ds_all[m, h])
+
+    run_scan(
+        True, False, part, (ds_ref,), state_ref, (ds_all,), scratch, 1,
+        lambda: None, early, late, lambda end: None,
+    )
+
+    @pl.loop(0, owned)
+    def _(h):
+        one, two = sketches(k_ref[h], proj, width)
+        s = one * two
+        feat = pair_features(s)
+        v = v_ref[h]
+        lanes = v.shape[1]
+        held = jnp.concatenate(
+            [state_ref[piece_of(part, h, j, per)] for j in range(per)], axis=0
+        ).astype(f32)
+        state = held[:pairs]
+        totals = unpack_totals(held[pairs:], pairs)
+        total_columns = jnp.concatenate([totals, jnp.zeros((lanes - 1, pairs), f32)], axis=0).T
+        cotangent = nt(
+            jnp.concatenate([state, total_columns], axis=1).astype(bf16), ones_beside(v)
+        )
+        ds = dsk_ref[h].T + pair_back(cotangent, s)
+        dk_ref[h] = finish(ds, one, two, proj, inverse).astype(bf16)
+        state_rows = doubled(state.T, width, 1).astype(bf16)
+        dvo_ref[h] = (dv_ref[h] + nn(state_rows, feat).T).astype(bf16)
+
+
+def pieces(heads, rows, lanes):
+    piece = heads * rows // TEAM
+    chunks = 2 if piece % 32 == 0 else 1
+    return (TEAM, chunks, piece // chunks, lanes)
+
+
+def scan_scratch(shape, swaps):
+    sides = max(lax.axis_size("head") - 1, 1)
+    chunks = shape[1]
+    sems = pltpu.SemaphoreType.DMA
+    one = pltpu.VMEM(shape[1:], bf16)
+    two = pltpu.VMEM((2,) + shape[1:], bf16)
+    return [
+        two, one, one, one, one, one, one, two,
+        sems((2, 2, chunks)),
+        sems((2, chunks)),
+        sems((2, chunks)),
+        sems((2, chunks)),
+        sems((2, 2, chunks)),
+        sems((swaps, sides)),
+        sems((swaps, sides)),
+        sems((swaps,)),
+    ]
+
+
+def call_scan(kernel, outs, in_specs, out_specs, scratch, number, args):
+    return pl.pallas_call(
+        kernel,
+        out_shape=outs,
+        in_specs=in_specs,
+        out_specs=out_specs,
+        scratch_shapes=scratch,
+        compiler_params=pltpu.CompilerParams(
+            collective_id=number, has_side_effects=True, vmem_limit_bytes=GRANT
+        ),
     )(*args)
 
 
@@ -240,22 +529,24 @@
     mine, _, tokens, hd = q.shape
     members = mine * lax.axis_size("head")
     shape = jax.ShapeDtypeStruct
-    sq, block_state = call(
+    shape_in = pieces(owned, rows, hd)
+    whole = pl.BlockSpec(memory_space=pltpu.VMEM)
+    apart = pl.BlockSpec(memory_space=pl.ANY)
+    state, sq, g = call_scan(
         first_kernel,
-        (shape((mine, heads_all, width, tokens), bf16), shape((owned, rows, hd), bf16)),
-        (q, k, v, proj),
-    )
-    sq = lax.all_to_all(sq, "head", split_axis=1, concat_axis=0, tiled=True)
-    g = lax.all_to_all(g, "head", split_axis=1, concat_axis=0, tiled=True)
-    count = lax.axis_size("ctx")
-    place = lax.axis_index("ctx")
-    source = lax.broadcasted_iota(jnp.int32, (count, 1, 1, 1), 0)
-
-    def scan(part, keep):
-        gathered = lax.all_gather(part, "ctx")
-        return jnp.sum(jnp.where(keep, gathered.astype(f32), 0.0), 0)
-
-    state = scan(block_state, source < place)
+        (
+            shape(shape_in, bf16),
+            shape((members, owned, 2 * width, tokens), bf16),
+            shape((members, owned, tokens, hd), bf16),
+        ),
+        [whole, whole, whole, apart, whole],
+        (whole, apart, apart),
+        [pltpu.VMEM(shape_in, bf16), pltpu.VMEM((mine, heads_all, 2 * width, tokens), bf16)]
+        + scan_scratch(shape_in, 2),
+        0,
+        (q, k, v, g, proj),
+    )
+    state = state.reshape(owned, rows, hd)
     by_member = lambda h: (0, h, 0, 0)
     by_head = lambda h: (h, 0, 0)
     dsq, dsk, dv, part = call(
@@ -269,7 +560,7 @@
         (sq, k, v, g, proj, state),
         grid=(owned,),
         in_specs=[
-            pl.BlockSpec((members, 1, width, tokens), by_member),
+            pl.BlockSpec((members, 1, 2 * width, tokens), by_member),
             pl.BlockSpec((1, tokens, hd), by_head),
             pl.BlockSpec((1, tokens, hd), by_head),
             pl.BlockSpec((members, 1, tokens, hd), by_member),
@@ -283,16 +574,19 @@
             pl.BlockSpec((1, rows, hd), by_head),
         ),
     )
-    dsq = lax.all_to_all(dsq, "head", split_axis=0, concat_axis=1, tiled=True)
-    later = scan(part, source > place)
-    dq, dk, dv = call(
+    dq, dk, dv = call_scan(
         last_kernel,
         (
             shape((mine, heads_all, tokens, hd), bf16),
             shape((owned, tokens, hd), bf16),
             shape((owned, tokens, hd), bf16),
         ),
-        (q, dsq, k, v, proj, later, dsk, dv),
+        [whole] * 8,
+        (whole,) * 3,
+        [pltpu.VMEM(shape_in, bf16), pltpu.VMEM((mine, heads_all, width, tokens), bf16)]
+        + scan_scratch(shape_in, 1),
+        1,
+        (part.reshape(shape_in), q, dsq, k, v, proj, dsk, dv),
     )
     return dq.transpose(2, 0, 1, 3), dk.transpose(1, 0, 2), dv.transpose(1, 0, 2)
 

time: 230 us -> 84.2 us (0.37)
  waiting for transfers between devices: 139 us -> 0 us
  Pallas kernels: 31 us -> 71.8 us
  between operations: 14.1 us -> 0.69 us
  other arithmetic: 13.6 us -> 0.71 us
  starting transfers between devices: 11.3 us -> 0 us
  local copies, waits for them, and re-layouts: 20.3 us -> 10.7 us
    all_gather x2 -> x0, waiting for transfers between devices: 118 us -> none  [scan(): gathered = lax.all_gather(part, 'ctx')]
    pallas_call x0 -> x2, Pallas kernels: none -> 59.8 us  [call_scan(): pl.pallas_call(kernel, out_shape=outs, in_specs=in_specs, out_specs=out_s...]
    all_to_all x3 -> x0, waiting for transfers between devices: 21.2 us -> none  [the longest x1 12.5 us: body(): g = lax.all_to_all(g, 'head', split_axis=1, concat_axis=0, tiled=True)]
    pallas_call x3 -> x1, Pallas kernels: 31 us -> 12.1 us  [call(): pl.pallas_call(kernel, out_shape=outs, compiler_params=pltpu.CompilerPara...]
    reduce_sum x2 -> x0, other arithmetic: 12.9 us -> none  [scan(): return jnp.sum(jnp.where(keep, gathered.astype(f32), 0.0), 0)]
    all_to_all x3 -> x0, starting transfers between devices: 11.3 us -> none  [the longest x1 4.23 us: body(): sq = lax.all_to_all(sq, 'head', split_axis=1, concat_axis=0, tiled=True)]
    unnamed x9 -> x17, local copies, waits for them, and re-layouts: 13.7 us -> 6.46 us
    all_to_all x3 -> x0, local copies, waits for them, and re-layouts: 2.67 us -> none  [the longest x1 1.17 us: body(): g = lax.all_to_all(g, 'head', split_axis=1, concat_axis=0, tiled=True)]
  transfers between devices with their start and end apart: 5 -> 0, of which waited for: 5 -> 0; matrix products, arithmetic and copies ran while one was open for 3% -> 0% of each run, Pallas kernels for 0% -> 0%
where the time goes in v3:
time: 84.2 us; the launch traced here: 83.9 us
  Pallas kernels  71.8 us (85%)
  local copies, waits for them, and re-layouts  10.7 us (13%)
    pallas_call x2, Pallas kernels, call_scan(): pl.pallas_call(kernel, out_shape=outs, in_specs=in_specs, out_specs=out_s...  59.8 us
    pallas_call x1, Pallas kernels, call(): pl.pallas_call(kernel, out_shape=outs, compiler_params=pltpu.CompilerPara...  12.1 us
    unnamed x17, local copies, waits for them, and re-layouts  6.46 us
    transpose x1, local copies, waits for them, and re-layouts, body(): g = dout.transpose(1, 2, 0, 3)  1.96 us

profile of v3, /device:TPU:0, one launch (start us, length us, event | category | flops | bytes accessed | tf_op | source)
XLA Modules:
  0.0 83.9 jit_solution(3643615153547831833)
XLA Ops:
  0.6 0.0 copy-start.4
  0.6 0.8 fusion.2
  1.4 0.1 copy.19
  1.5 0.1 copy.20
  1.7 0.7 pad_maximum_fusion.proj_ref
  2.4 0.0 copy-done.4
  2.4 0.0 copy-start
  2.4 0.0 copy-start.1
  2.4 1.5 %constant_dynamic-slice_fusion = (bf16[256,4,128]{2,1,0:T(4,128)(2,1)S(1)}, bf16[256,4,128]{2,1,0:T(4,128)(2,1)S(1)}) fusion(bf16[256,8,128]{2,1,0:T(8,128)(2,1)S(1)} %copy-done.4, s32[]{:T(128)S(6)} %select_n.4, bf16[256,8,128]{2,1,0:T(8,128)(2,1)} %param.6), kind=kLoop, calls=%fused_computation.9 | loop fusion | bytes 1048580 | tf_op jit(solution)/shard_map/dynamic_slice | solution.py:526
  3.8 0.7 copy.25
  4.6 0.7 copy.26
  5.3 0.0 copy-done
  5.3 0.0 copy-done.1
  5.3 2.0 %copy_bitcast_fusion = (bf16[2,8,256,128]{3,2,1,0:T(8,128)(2,1)}, bf16[2,8,256,128]{3,2,1,0:T(8,128)(2,1)}) fusion(bf16[256,2,8,128]{3,2,1,0:T(8,128)(2,1)S(1)} %copy-done, bf16[256,2,8,128]{3,2,1,0:T(8,128)(2,1)S(1)} %copy-done.1), kind=kLoop, calls=%fused_computation | loop fusion | bytes 4194304 | tf_op jit(solution)/shard_map/transpose | solution.py:528
  7.3 26.6 %shard_map.76 = (bf16[4,2,272,128]{3,2,1,0:T(8,128)(2,1)}, bf16[4,4,64,256]{3,2,1,0:T(8,128)(2,1)}, bf16[4,4,256,128]{3,2,1,0:T(8,128)(2,1)}) custom-call(bf16[2,8,256,128]{3,2,1,0:T(8,128)(2,1)} %get-tuple-element.33.q_ref, bf16[4,256,128]{2,1,0:T(8,128)(2,1)} %bitcast.22, bf16[4,256,128]{2,1,0:T(8,128)(2,1)} %bitcast.19, ...), custom_call_target="tpu_custom_call" | custom-call | tf_op jit(solution)/shard_map/pallas_call | solution.py:505
  33.9 12.1 %shard_map.77 = (bf16[4,4,32,256]{3,2,1,0:T(8,128)(2,1)}, f32[4,256,32]{2,1,0:T(8,128)}, f32[4,256,128]{2,1,0:T(8,128)}, bf16[4,544,128]{2,1,0:T(8,128)(2,1)}) custom-call(bf16[4,4,64,256]{3,2,1,0:T(8,128)(2,1)} %get-tuple-element.13.sq_ref, bf16[4,256,128]{2,1,0:T(8,128)(2,1)} %bitcast.23, bf16[4,256,128]{2,1,0:T(8,128)(2,1)} %bitcast.20, ...), custom_call_target="tpu_custom_call" | custom-call | tf_op jit(solution)/shard_map/pallas_call | solution.py:171
  46.0 33.1 %shard_map.78 = (bf16[2,8,256,128]{3,2,1,0:T(8,128)(2,1)}, bf16[4,256,128]{2,1,0:T(8,128)(2,1)}, bf16[4,256,128]{2,1,0:T(8,128)(2,1)}) custom-call(bf16[4,2,272,128]{3,2,1,0:T(8,128)(2,1)} %bitcast.26, bf16[2,8,256,128]{3,2,1,0:T(8,128)(2,1)} %get-tuple-element.33.q_ref, bf16[4,4,32,256]{3,2,1,0:T(8,128)(2,1)} %get-tuple-element.17.ds_ref, ...), custom_call_target="tpu_custom_call" | custom-call | tf_op jit(solution)/shard_map/pallas_call | solution.py:505
  79.1 0.0 copy-start.3
  79.1 2.9 %copy.14 = bf16[256,2,8,128]{3,2,1,0:T(8,128)(2,1)} copy(bf16[256,2,8,128]{3,0,2,1:T(8,128)(2,1)} %bitcast.25) | data formatting | bytes 2097152
  82.0 0.0 copy-done.3
  82.0 0.0 copy-start.2
  82.0 0.9 %copy.15 = bf16[256,4,128]{2,1,0:T(4,128)(2,1)} copy(bf16[256,4,128]{2,0,1:T(8,128)(2,1)S(1)} %bitcast.29) | data formatting | bytes 524288
  82.9 0.0 copy-done.2
  83.0 0.9 %copy.16 = bf16[256,4,128]{2,1,0:T(4,128)(2,1)} copy(bf16[256,4,128]{2,0,1:T(8,128)(2,1)S(1)} %bitcast.28) | data formatting | bytes 524288
  (1 shorter events, 0.0 us)
Async XLA Ops:
  0.6 1.7 %copy-start.4 = (bf16[256,8,128]{2,1,0:T(8,128)(2,1)S(1)}, bf16[256,8,128]{2,1,0:T(8,128)(2,1)}, u32[]{:S(2)}) copy-start(bf16[256,8,128]{2,1,0:T(8,128)(2,1)} %param.7) | copy-start | bytes 1572868
  2.4 2.9 %copy-start = (bf16[256,2,8,128]{3,2,1,0:T(8,128)(2,1)S(1)}, bf16[256,2,8,128]{3,2,1,0:T(8,128)(2,1)}, u32[]{:S(2)}) copy-start(bf16[256,2,8,128]{3,2,1,0:T(8,128)(2,1)} %param.8) | copy-start | bytes 3145732
  2.4 2.9 %copy-start.1 = (bf16[256,2,8,128]{3,2,1,0:T(8,128)(2,1)S(1)}, bf16[256,2,8,128]{3,2,1,0:T(8,128)(2,1)}, u32[]{:S(2)}) copy-start(bf16[256,2,8,128]{3,2,1,0:T(8,128)(2,1)} %param.5) | copy-start | bytes 3145732
  79.1 2.9 %copy-start.3 = (bf16[4,256,128]{2,1,0:T(8,128)(2,1)S(1)}, bf16[4,256,128]{2,1,0:T(8,128)(2,1)}, u32[]{:S(2)}) copy-start(bf16[4,256,128]{2,1,0:T(8,128)(2,1)} %get-tuple-element.21) | copy-start | bytes 786436
  82.0 1.0 %copy-start.2 = (bf16[4,256,128]{2,1,0:T(8,128)(2,1)S(1)}, bf16[4,256,128]{2,1,0:T(8,128)(2,1)}, u32[]{:S(2)}) copy-start(bf16[4,256,128]{2,1,0:T(8,128)(2,1)} %get-tuple-element.22) | copy-start | bytes 786436

commit v4 on v3

--- a/solution.py
+++ b/solution.py
@@ -70,7 +70,7 @@
     return dot(jnp.concatenate([high, low], axis=0), both, ((0,), (1,))) * scale
 
 
-def pack_totals(column, lanes):
+def pack_totals(column, lanes, depth):
     count = column.shape[0]
     row = column.T[:1]
     rows = []
@@ -81,7 +81,7 @@
                 [piece, jnp.zeros((1, lanes - piece.shape[1]), f32)], axis=1
             )
         rows.append(piece)
-    rows.append(jnp.zeros((16 - len(rows), lanes), f32))
+    rows.append(jnp.zeros((depth - len(rows), lanes), f32))
     return jnp.concatenate(rows, axis=0)
 
 
@@ -96,8 +96,9 @@
     return jnp.concatenate([v, jnp.where(lane == 0, 1.0, 0.0).astype(bf16)], axis=1)
 
 
-def state_with_totals(wide, lanes):
-    return jnp.concatenate([wide[:, :lanes], pack_totals(wide[:, lanes:], lanes)], axis=0)
+def state_with_totals(wide, lanes, rows):
+    packed = pack_totals(wide[:, lanes:], lanes, rows - wide.shape[0])
+    return jnp.concatenate([wide[:, :lanes], packed], axis=0)
 
 
 def main_kernel(
@@ -162,9 +163,8 @@
 
     wide = nt(feat, spread)
     both = wide[:, lanes:] + pltpu.roll(wide[:, lanes:], lanes - 1, 1)
-    out_ref[0] = state_with_totals(jnp.concatenate([wide[:, :lanes], both], axis=1), lanes).astype(
-        bf16
-    )
+    kept = jnp.concatenate([wide[:, :lanes], both], axis=1)
+    out_ref[0] = state_with_totals(kept, lanes, out_ref.shape[1]).astype(bf16)
 
 
 def call(kernel, outs, args, **more):
@@ -177,6 +177,7 @@
 
 
 TEAM = 4
+CHUNK = 144
 
 
 def run_scan(reverse, spread, part, sources, out, targets, scratch, ready, fill, early, late, final):
@@ -323,11 +324,18 @@
         chip[c] = (wide(part, 2 * (1 - x) + core, c) + wide(mate, 1 - x, c)).astype(bf16)
         to_chip(c).start()
 
-    early()
-    for n in range(ready, swaps):
-        begin(n)
-
-    @pl.when(has_last)
+    passed = groups - 1 - group if reverse else group
+
+    def first_part():
+        early()
+        for n in range(ready, swaps):
+            begin(n)
+
+    @pl.when(passed >= 1)
+    def _():
+        first_part()
+
+    @pl.when(passed >= 2)
     def _():
         late(end)
 
@@ -356,7 +364,11 @@
         to_base(c).start()
         deliver(x, c, before + there * late_x)
 
-    @pl.when(jnp.logical_not(has_last))
+    @pl.when(passed < 1)
+    def _():
+        first_part()
+
+    @pl.when(passed < 2)
     def _():
         late(end)
 
@@ -396,7 +408,7 @@
             one, two = sketches(k_ref[h], proj, width)
             v = v_ref[h]
             wide = nn(pair_features(one * two), ones_beside(v))
-            state = state_with_totals(wide, v.shape[1]).astype(bf16)
+            state = state_with_totals(wide, v.shape[1], per * rows).astype(bf16)
             for j in range(per):
                 part[piece_of(part, h, j, per)] = state[j * rows : (j + 1) * rows]
 
@@ -478,7 +490,7 @@
 
 def pieces(heads, rows, lanes):
     piece = heads * rows // TEAM
-    chunks = 2 if piece % 32 == 0 else 1
+    chunks = piece // CHUNK if piece % CHUNK == 0 else 1
     return (TEAM, chunks, piece // chunks, lanes)
 
 
@@ -518,7 +530,7 @@
     proj = jnp.concatenate([2 * signs[0] - 1, 2 * signs[1] - 1], axis=1).astype(bf16)
     width = signs.shape[-1]
     pairs = pair_count(width)
-    rows = pairs + 16
+    rows = -(-(pairs + 16) // CHUNK) * CHUNK
     heads_all = keys.shape[1]
     owned = heads_all // lax.axis_size("head")
     offset = lax.axis_index("head") * owned

time: 84.2 us -> 79.9 us (0.949)
  Pallas kernels: 71.8 us -> 67.5 us
    pallas_call x2, Pallas kernels: 59.8 us -> 55.4 us  [call_scan(): pl.pallas_call(kernel, out_shape=outs, in_specs=in_specs, out_specs=out_s...]
where the time goes in v4:
time: 79.9 us; the launch traced here: 79.6 us
  Pallas kernels  67.5 us (84%)
  local copies, waits for them, and re-layouts  10.7 us (13%)
    pallas_call x2, Pallas kernels, call_scan(): pl.pallas_call(kernel, out_shape=outs, in_specs=in_specs, out_specs=out_s...  55.4 us
    pallas_call x1, Pallas kernels, call(): pl.pallas_call(kernel, out_shape=outs, compiler_params=pltpu.CompilerPara...  12.1 us
    unnamed x17, local copies, waits for them, and re-layouts  6.46 us
    transpose x1, local copies, waits for them, and re-layouts, body(): g = dout.transpose(1, 2, 0, 3)  1.96 us

profile of v4, /device:TPU:0, one launch (start us, length us, event | category | flops | bytes accessed | tf_op | source)
XLA Modules:
  0.0 79.6 jit_solution(17051747135081608488)
XLA Ops:
  0.6 0.0 copy-start.4
  0.6 0.8 fusion.2
  1.4 0.1 copy.19
  1.5 0.1 copy.20
  1.7 0.7 pad_maximum_fusion.proj_ref
  2.4 0.0 copy-done.4
  2.4 0.0 copy-start
  2.4 0.0 copy-start.1
  2.4 1.5 %constant_dynamic-slice_fusion = (bf16[256,4,128]{2,1,0:T(4,128)(2,1)S(1)}, bf16[256,4,128]{2,1,0:T(4,128)(2,1)S(1)}) fusion(bf16[256,8,128]{2,1,0:T(8,128)(2,1)S(1)} %copy-done.4, s32[]{:T(128)S(6)} %select_n.4, bf16[256,8,128]{2,1,0:T(8,128)(2,1)} %param.6), kind=kLoop, calls=%fused_computation.9 | loop fusion | bytes 1048580 | tf_op jit(solution)/shard_map/dynamic_slice | solution.py:538
  3.8 0.7 copy.25
  4.6 0.7 copy.26
  5.3 0.0 copy-done
  5.3 0.0 copy-done.1
  5.3 2.0 %copy_bitcast_fusion = (bf16[2,8,256,128]{3,2,1,0:T(8,128)(2,1)}, bf16[2,8,256,128]{3,2,1,0:T(8,128)(2,1)}) fusion(bf16[256,2,8,128]{3,2,1,0:T(8,128)(2,1)S(1)} %copy-done, bf16[256,2,8,128]{3,2,1,0:T(8,128)(2,1)S(1)} %copy-done.1), kind=kLoop, calls=%fused_computation | loop fusion | bytes 4194304 | tf_op jit(solution)/shard_map/transpose | solution.py:540
  7.3 27.7 %shard_map.76 = (bf16[4,4,144,128]{3,2,1,0:T(8,128)(2,1)}, bf16[4,4,64,256]{3,2,1,0:T(8,128)(2,1)}, bf16[4,4,256,128]{3,2,1,0:T(8,128)(2,1)}) custom-call(bf16[2,8,256,128]{3,2,1,0:T(8,128)(2,1)} %get-tuple-element.33.q_ref, bf16[4,256,128]{2,1,0:T(8,128)(2,1)} %bitcast.22, bf16[4,256,128]{2,1,0:T(8,128)(2,1)} %bitcast.19, ...), custom_call_target="tpu_custom_call" | custom-call | tf_op jit(solution)/shard_map/pallas_call | solution.py:517
  35.0 12.1 %shard_map.77 = (bf16[4,4,32,256]{3,2,1,0:T(8,128)(2,1)}, f32[4,256,32]{2,1,0:T(8,128)}, f32[4,256,128]{2,1,0:T(8,128)}, bf16[4,576,128]{2,1,0:T(8,128)(2,1)}) custom-call(bf16[4,4,64,256]{3,2,1,0:T(8,128)(2,1)} %get-tuple-element.13.sq_ref, bf16[4,256,128]{2,1,0:T(8,128)(2,1)} %bitcast.23, bf16[4,256,128]{2,1,0:T(8,128)(2,1)} %bitcast.20, ...), custom_call_target="tpu_custom_call" | custom-call | tf_op jit(solution)/shard_map/pallas_call | solution.py:171
  47.1 27.8 %shard_map.78 = (bf16[2,8,256,128]{3,2,1,0:T(8,128)(2,1)}, bf16[4,256,128]{2,1,0:T(8,128)(2,1)}, bf16[4,256,128]{2,1,0:T(8,128)(2,1)}) custom-call(bf16[4,4,144,128]{3,2,1,0:T(8,128)(2,1)} %bitcast.26, bf16[2,8,256,128]{3,2,1,0:T(8,128)(2,1)} %get-tuple-element.33.q_ref, bf16[4,4,32,256]{3,2,1,0:T(8,128)(2,1)} %get-tuple-element.17.ds_ref, ...), custom_call_target="tpu_custom_call" | custom-call | tf_op jit(solution)/shard_map/pallas_call | solution.py:517
  74.8 0.0 copy-start.3
  74.8 2.9 %copy.14 = bf16[256,2,8,128]{3,2,1,0:T(8,128)(2,1)} copy(bf16[256,2,8,128]{3,0,2,1:T(8,128)(2,1)} %bitcast.25) | data formatting | bytes 2097152
  77.8 0.0 copy-done.3
  77.8 0.0 copy-start.2
  77.8 0.9 %copy.15 = bf16[256,4,128]{2,1,0:T(4,128)(2,1)} copy(bf16[256,4,128]{2,0,1:T(8,128)(2,1)S(1)} %bitcast.29) | data formatting | bytes 524288
  78.7 0.0 copy-done.2
  78.7 0.9 %copy.16 = bf16[256,4,128]{2,1,0:T(4,128)(2,1)} copy(bf16[256,4,128]{2,0,1:T(8,128)(2,1)S(1)} %bitcast.28) | data formatting | bytes 524288
  (1 shorter events, 0.0 us)
Async XLA Ops:
  0.6 1.7 %copy-start.4 = (bf16[256,8,128]{2,1,0:T(8,128)(2,1)S(1)}, bf16[256,8,128]{2,1,0:T(8,128)(2,1)}, u32[]{:S(2)}) copy-start(bf16[256,8,128]{2,1,0:T(8,128)(2,1)} %param.7) | copy-start | bytes 1572868
  2.4 2.9 %copy-start = (bf16[256,2,8,128]{3,2,1,0:T(8,128)(2,1)S(1)}, bf16[256,2,8,128]{3,2,1,0:T(8,128)(2,1)}, u32[]{:S(2)}) copy-start(bf16[256,2,8,128]{3,2,1,0:T(8,128)(2,1)} %param.8) | copy-start | bytes 3145732
  2.4 2.9 %copy-start.1 = (bf16[256,2,8,128]{3,2,1,0:T(8,128)(2,1)S(1)}, bf16[256,2,8,128]{3,2,1,0:T(8,128)(2,1)}, u32[]{:S(2)}) copy-start(bf16[256,2,8,128]{3,2,1,0:T(8,128)(2,1)} %param.5) | copy-start | bytes 3145732
  74.8 2.9 %copy-start.3 = (bf16[4,256,128]{2,1,0:T(8,128)(2,1)S(1)}, bf16[4,256,128]{2,1,0:T(8,128)(2,1)}, u32[]{:S(2)}) copy-start(bf16[4,256,128]{2,1,0:T(8,128)(2,1)} %get-tuple-element.21) | copy-start | bytes 786436
  77.8 1.0 %copy-start.2 = (bf16[4,256,128]{2,1,0:T(8,128)(2,1)S(1)}, bf16[4,256,128]{2,1,0:T(8,128)(2,1)}, u32[]{:S(2)}) copy-start(bf16[4,256,128]{2,1,0:T(8,128)(2,1)} %get-tuple-element.22) | copy-start | bytes 786436

commit v5 on v4

--- a/solution.py
+++ b/solution.py
@@ -26,8 +26,12 @@
     return width * width // 2 + width // 2
 
 
+def projector(sign_ref):
+    return (2 * sign_ref[...] - 1).astype(f32).astype(bf16)
+
+
 def sketches(tokens, proj, width):
-    both = dot(proj, tokens, ((0,), (1,))) * tokens.shape[-1] ** (-0.5)
+    both = nt(proj, tokens) * tokens.shape[-1] ** (-0.5)
     return both[:width], both[width:]
 
 
@@ -66,8 +70,8 @@
 
 def finish(ds, one, two, proj, scale):
     high, low = split(jnp.concatenate([ds * two, ds * one], axis=0))
-    both = jnp.concatenate([proj, proj], axis=1)
-    return dot(jnp.concatenate([high, low], axis=0), both, ((0,), (1,))) * scale
+    both = jnp.concatenate([proj, proj], axis=0)
+    return dot(jnp.concatenate([high, low], axis=0), both, ((0,), (0,))) * scale
 
 
 def pack_totals(column, lanes, depth):
@@ -102,10 +106,10 @@
 
 
 def main_kernel(
-    sq_ref, k_ref, v_ref, g_ref, proj_ref, state_ref, dsq_ref, dsk_ref, dv_ref, out_ref
+    sq_ref, k_ref, v_ref, g_ref, sign_ref, state_ref, dsq_ref, dsk_ref, dv_ref, out_ref
 ):
-    proj = proj_ref[...]
-    width = proj.shape[1] // 2
+    proj = projector(sign_ref)
+    width = proj.shape[0] // 2
     pairs = pair_count(width)
     members = sq_ref.shape[0]
     tokens, lanes = v_ref.shape[1:]
@@ -395,9 +399,9 @@
     return at // buffer.shape[1], lax.rem(at, buffer.shape[1])
 
 
-def first_kernel(q_ref, k_ref, v_ref, g_ref, proj_ref, out, s_out, g_out, part, s_held, *scratch):
-    proj = proj_ref[...]
-    width = proj.shape[1] // 2
+def first_kernel(q_ref, k_ref, v_ref, g_ref, sign_ref, out, s_out, g_out, part, s_held, *scratch):
+    proj = projector(sign_ref)
+    width = proj.shape[0] // 2
     owned = k_ref.shape[0]
     per = part.shape[0] * part.shape[1] // owned
     rows = part.shape[2]
@@ -428,11 +432,11 @@
 
 
 def last_kernel(
-    part, q_ref, ds_ref, k_ref, v_ref, proj_ref, dsk_ref, dv_ref, dq_ref, dk_ref, dvo_ref,
+    part, q_ref, ds_ref, k_ref, v_ref, sign_ref, dsk_ref, dv_ref, dq_ref, dk_ref, dvo_ref,
     state_ref, ds_all, *scratch,
 ):
-    proj = proj_ref[...]
-    width = proj.shape[1] // 2
+    proj = projector(sign_ref)
+    width = proj.shape[0] // 2
     pairs = pair_count(width)
     owned = k_ref.shape[0]
     per = part.shape[0] * part.shape[1] // owned
@@ -527,7 +531,7 @@
 
 
 def body(queries, keys, values, dout, signs):
-    proj = jnp.concatenate([2 * signs[0] - 1, 2 * signs[1] - 1], axis=1).astype(bf16)
+    sign_rows = signs.transpose(0, 2, 1).reshape(-1, signs.shape[1])
     width = signs.shape[-1]
     pairs = pair_count(width)
     rows = -(-(pairs + 16) // CHUNK) * CHUNK
@@ -556,7 +560,7 @@
         [pltpu.VMEM(shape_in, bf16), pltpu.VMEM((mine, heads_all, 2 * width, tokens), bf16)]
         + scan_scratch(shape_in, 2),
         0,
-        (q, k, v, g, proj),
+        (q, k, v, g, sign_rows),
     )
     state = state.reshape(owned, rows, hd)
     by_member = lambda h: (0, h, 0, 0)
@@ -569,14 +573,14 @@
             shape((owned, tokens, hd), f32),
             shape((owned, rows, hd), bf16),
         ),
-        (sq, k, v, g, proj, state),
+        (sq, k, v, g, sign_rows, state),
         grid=(owned,),
         in_specs=[
             pl.BlockSpec((members, 1, 2 * width, tokens), by_member),
             pl.BlockSpec((1, tokens, hd), by_head),
             pl.BlockSpec((1, tokens, hd), by_head),
             pl.BlockSpec((members, 1, tokens, hd), by_member),
-            pl.BlockSpec((hd, 2 * width), lambda h: (0, 0)),
+            pl.BlockSpec((2 * width, hd), lambda h: (0, 0)),
             pl.BlockSpec((1, rows, hd), by_head),
         ],
         out_specs=(
@@ -598,7 +602,7 @@
         [pltpu.VMEM(shape_in, bf16), pltpu.VMEM((mine, heads_all, width, tokens), bf16)]
         + scan_scratch(shape_in, 1),
         1,
-        (part.reshape(shape_in), q, dsq, k, v, proj, dsk, dv),
+        (part.reshape(shape_in), q, dsq, k, v, sign_rows, dsk, dv),
     )
     return dq.transpose(2, 0, 1, 3), dk.transpose(1, 0, 2), dv.transpose(1, 0, 2)
 

time: 79.9 us -> 77.8 us (0.974)
  local copies, waits for them, and re-layouts: 10.7 us -> 9.84 us
    unnamed x17 -> x13, local copies, waits for them, and re-layouts: 6.46 us -> 6.26 us
where the time goes in v5:
time: 77.8 us; the launch traced here: 77.6 us
  Pallas kernels  67.1 us (86%)
  local copies, waits for them, and re-layouts  9.84 us (13%)
    pallas_call x2, Pallas kernels, call_scan(): pl.pallas_call(kernel, out_shape=outs, in_specs=in_specs, out_specs=out_s...  55 us
    pallas_call x1, Pallas kernels, call(): pl.pallas_call(kernel, out_shape=outs, compiler_params=pltpu.CompilerPara...  12.1 us
    unnamed x13, local copies, waits for them, and re-layouts  6.26 us
    transpose x1, local copies, waits for them, and re-layouts, body(): g = dout.transpose(1, 2, 0, 3)  1.95 us
    dynamic_slice x1, local copies, waits for them, and re-layouts, body(): v = lax.dynamic_slice_in_dim(values, offset, owned, 1).transpose(1, 0, 2)  1.62 us

profile of v5, /device:TPU:0, one launch (start us, length us, event | category | flops | bytes accessed | tf_op | source)
XLA Modules:
  0.0 77.6 jit_solution(15907820390934416791)
XLA Ops:
  0.6 0.0 copy-start
  0.6 0.0 copy-start.1
  0.7 1.6 %constant_dynamic-slice_fusion = (bf16[256,4,128]{2,1,0:T(4,128)(2,1)S(1)}, bf16[256,4,128]{2,1,0:T(4,128)(2,1)S(1)}) fusion(bf16[256,8,128]{2,1,0:T(8,128)(2,1)} %param.7, s32[]{:T(128)S(6)} %select_n.4, bf16[256,8,128]{2,1,0:T(8,128)(2,1)} %param.6), kind=kLoop, calls=%fused_computation.4 | loop fusion | bytes 1048580 | tf_op jit(solution)/shard_map/dynamic_slice | solution.py:542
  2.3 0.7 copy.21
  3.0 0.7 copy.22
  3.8 0.0 copy-done
  3.8 0.0 copy-done.1
  3.8 2.0 %copy_bitcast_fusion = (bf16[2,8,256,128]{3,2,1,0:T(8,128)(2,1)}, bf16[2,8,256,128]{3,2,1,0:T(8,128)(2,1)}) fusion(bf16[256,2,8,128]{3,2,1,0:T(8,128)(2,1)S(1)} %copy-done, bf16[256,2,8,128]{3,2,1,0:T(8,128)(2,1)S(1)} %copy-done.1), kind=kLoop, calls=%fused_computation | loop fusion | bytes 4194304 | tf_op jit(solution)/shard_map/transpose | solution.py:544
  5.7 27.2 %shard_map.76 = (bf16[4,4,144,128]{3,2,1,0:T(8,128)(2,1)}, bf16[4,4,64,256]{3,2,1,0:T(8,128)(2,1)}, bf16[4,4,256,128]{3,2,1,0:T(8,128)(2,1)}) custom-call(bf16[2,8,256,128]{3,2,1,0:T(8,128)(2,1)} %get-tuple-element.29.q_ref, bf16[4,256,128]{2,1,0:T(8,128)(2,1)} %bitcast.21, bf16[4,256,128]{2,1,0:T(8,128)(2,1)} %bitcast.18, ...), custom_call_target="tpu_custom_call" | custom-call | tf_op jit(solution)/shard_map/pallas_call | solution.py:521
  33.0 12.1 %shard_map.77 = (bf16[4,4,32,256]{3,2,1,0:T(8,128)(2,1)}, f32[4,256,32]{2,1,0:T(8,128)}, f32[4,256,128]{2,1,0:T(8,128)}, bf16[4,576,128]{2,1,0:T(8,128)(2,1)}) custom-call(bf16[4,4,64,256]{3,2,1,0:T(8,128)(2,1)} %get-tuple-element.13.sq_ref, bf16[4,256,128]{2,1,0:T(8,128)(2,1)} %bitcast.22, bf16[4,256,128]{2,1,0:T(8,128)(2,1)} %bitcast.19, ...), custom_call_target="tpu_custom_call" | custom-call | tf_op jit(solution)/shard_map/pallas_call | solution.py:175
  45.0 27.8 %shard_map.78 = (bf16[2,8,256,128]{3,2,1,0:T(8,128)(2,1)}, bf16[4,256,128]{2,1,0:T(8,128)(2,1)}, bf16[4,256,128]{2,1,0:T(8,128)(2,1)}) custom-call(bf16[4,4,144,128]{3,2,1,0:T(8,128)(2,1)} %bitcast.25, bf16[2,8,256,128]{3,2,1,0:T(8,128)(2,1)} %get-tuple-element.29.q_ref, bf16[4,4,32,256]{3,2,1,0:T(8,128)(2,1)} %get-tuple-element.17.ds_ref, ...), custom_call_target="tpu_custom_call" | custom-call | tf_op jit(solution)/shard_map/pallas_call | solution.py:521
  72.8 0.0 copy-start.3
  72.8 2.9 %copy.12 = bf16[256,2,8,128]{3,2,1,0:T(8,128)(2,1)} copy(bf16[256,2,8,128]{3,0,2,1:T(8,128)(2,1)} %bitcast.24) | data formatting | bytes 2097152
  75.7 0.0 copy-done.3
  75.7 0.0 copy-start.2
  75.7 0.9 %copy.13 = bf16[256,4,128]{2,1,0:T(4,128)(2,1)} copy(bf16[256,4,128]{2,0,1:T(8,128)(2,1)S(1)} %bitcast.31) | data formatting | bytes 524288
  76.6 0.0 copy-done.2
  76.7 0.9 %copy.14 = bf16[256,4,128]{2,1,0:T(4,128)(2,1)} copy(bf16[256,4,128]{2,0,1:T(8,128)(2,1)S(1)} %bitcast.30) | data formatting | bytes 524288
Async XLA Ops:
  0.6 3.1 %copy-start = (bf16[256,2,8,128]{3,2,1,0:T(8,128)(2,1)S(1)}, bf16[256,2,8,128]{3,2,1,0:T(8,128)(2,1)}, u32[]{:S(2)}) copy-start(bf16[256,2,8,128]{3,2,1,0:T(8,128)(2,1)} %param.8) | copy-start | bytes 3145732
  0.6 3.1 %copy-start.1 = (bf16[256,2,8,128]{3,2,1,0:T(8,128)(2,1)S(1)}, bf16[256,2,8,128]{3,2,1,0:T(8,128)(2,1)}, u32[]{:S(2)}) copy-start(bf16[256,2,8,128]{3,2,1,0:T(8,128)(2,1)} %param.5) | copy-start | bytes 3145732
  72.8 2.9 %copy-start.3 = (bf16[4,256,128]{2,1,0:T(8,128)(2,1)S(1)}, bf16[4,256,128]{2,1,0:T(8,128)(2,1)}, u32[]{:S(2)}) copy-start(bf16[4,256,128]{2,1,0:T(8,128)(2,1)} %get-tuple-element.21) | copy-start | bytes 786436
  75.7 1.0 %copy-start.2 = (bf16[4,256,128]{2,1,0:T(8,128)(2,1)S(1)}, bf16[4,256,128]{2,1,0:T(8,128)(2,1)}, u32[]{:S(2)}) copy-start(bf16[4,256,128]{2,1,0:T(8,128)(2,1)} %get-tuple-element.22) | copy-start | bytes 786436

commit v6 on v5

--- a/solution.py
+++ b/solution.py
@@ -538,8 +538,8 @@
     heads_all = keys.shape[1]
     owned = heads_all // lax.axis_size("head")
     offset = lax.axis_index("head") * owned
-    k = lax.dynamic_slice_in_dim(keys, offset, owned, 1).transpose(1, 0, 2)
-    v = lax.dynamic_slice_in_dim(values, offset, owned, 1).transpose(1, 0, 2)
+    k = lax.dynamic_slice_in_dim(keys.transpose(1, 0, 2), offset, owned, 0)
+    v = lax.dynamic_slice_in_dim(values.transpose(1, 0, 2), offset, owned, 0)
     q = queries.transpose(1, 2, 0, 3)
     g = dout.transpose(1, 2, 0, 3)
     mine, _, tokens, hd = q.shape

time: 77.8 us -> 77.8 us (level)
    another operation x0 -> x1, local copies, waits for them, and re-layouts: none -> 1.62 us
    dynamic_slice x1 -> x0, local copies, waits for them, and re-layouts: 1.62 us -> none  [body(): v = lax.dynamic_slice_in_dim(values, offset, owned, 1).transpose(1, 0, 2)]
where the time goes in v6:
time: 77.8 us; the launch traced here: 77.6 us
  Pallas kernels  67.1 us (86%)
  local copies, waits for them, and re-layouts  9.84 us (13%)
    pallas_call x2, Pallas kernels, call_scan(): pl.pallas_call(kernel, out_shape=outs, in_specs=in_specs, out_specs=out_s...  55 us
    pallas_call x1, Pallas kernels, call(): pl.pallas_call(kernel, out_shape=outs, compiler_params=pltpu.CompilerPara...  12.1 us
    unnamed x13, local copies, waits for them, and re-layouts  6.26 us
    transpose x1, local copies, waits for them, and re-layouts, body(): g = dout.transpose(1, 2, 0, 3)  1.95 us
    another operation x1, local copies, waits for them, and re-layouts  1.62 us

profile of v6, /device:TPU:0, one launch (start us, length us, event | category | flops | bytes accessed | tf_op | source)
XLA Modules:
  0.0 77.6 jit_solution(15907820390934416791)
XLA Ops:
  0.6 0.0 copy-start
  0.6 0.0 copy-start.1
  0.7 1.6 %constant_dynamic-slice_fusion = (bf16[256,4,128]{2,1,0:T(4,128)(2,1)S(1)}, bf16[256,4,128]{2,1,0:T(4,128)(2,1)S(1)}) fusion(bf16[256,8,128]{2,1,0:T(8,128)(2,1)} %param.7, s32[]{:T(128)S(6)} %select_n.4, bf16[256,8,128]{2,1,0:T(8,128)(2,1)} %param.6), kind=kLoop, calls=%fused_computation.4 | loop fusion | bytes 1048580 | tf_op jit(solution)/shard_map/dynamic-slice.1
  2.3 0.7 copy.21
  3.0 0.7 copy.22
  3.8 0.0 copy-done
  3.8 0.0 copy-done.1
  3.8 2.0 %copy_bitcast_fusion = (bf16[2,8,256,128]{3,2,1,0:T(8,128)(2,1)}, bf16[2,8,256,128]{3,2,1,0:T(8,128)(2,1)}) fusion(bf16[256,2,8,128]{3,2,1,0:T(8,128)(2,1)S(1)} %copy-done, bf16[256,2,8,128]{3,2,1,0:T(8,128)(2,1)S(1)} %copy-done.1), kind=kLoop, calls=%fused_computation | loop fusion | bytes 4194304 | tf_op jit(solution)/shard_map/transpose | solution.py:544
  5.7 27.2 %shard_map.76 = (bf16[4,4,144,128]{3,2,1,0:T(8,128)(2,1)}, bf16[4,4,64,256]{3,2,1,0:T(8,128)(2,1)}, bf16[4,4,256,128]{3,2,1,0:T(8,128)(2,1)}) custom-call(bf16[2,8,256,128]{3,2,1,0:T(8,128)(2,1)} %get-tuple-element.29.q_ref, bf16[4,256,128]{2,1,0:T(8,128)(2,1)} %bitcast.21, bf16[4,256,128]{2,1,0:T(8,128)(2,1)} %bitcast.18, ...), custom_call_target="tpu_custom_call" | custom-call | tf_op jit(solution)/shard_map/pallas_call | solution.py:521
  33.0 12.1 %shard_map.77 = (bf16[4,4,32,256]{3,2,1,0:T(8,128)(2,1)}, f32[4,256,32]{2,1,0:T(8,128)}, f32[4,256,128]{2,1,0:T(8,128)}, bf16[4,576,128]{2,1,0:T(8,128)(2,1)}) custom-call(bf16[4,4,64,256]{3,2,1,0:T(8,128)(2,1)} %get-tuple-element.13.sq_ref, bf16[4,256,128]{2,1,0:T(8,128)(2,1)} %bitcast.22, bf16[4,256,128]{2,1,0:T(8,128)(2,1)} %bitcast.19, ...), custom_call_target="tpu_custom_call" | custom-call | tf_op jit(solution)/shard_map/pallas_call | solution.py:175
  45.0 27.8 %shard_map.78 = (bf16[2,8,256,128]{3,2,1,0:T(8,128)(2,1)}, bf16[4,256,128]{2,1,0:T(8,128)(2,1)}, bf16[4,256,128]{2,1,0:T(8,128)(2,1)}) custom-call(bf16[4,4,144,128]{3,2,1,0:T(8,128)(2,1)} %bitcast.25, bf16[2,8,256,128]{3,2,1,0:T(8,128)(2,1)} %get-tuple-element.29.q_ref, bf16[4,4,32,256]{3,2,1,0:T(8,128)(2,1)} %get-tuple-element.17.ds_ref, ...), custom_call_target="tpu_custom_call" | custom-call | tf_op jit(solution)/shard_map/pallas_call | solution.py:521
  72.8 0.0 copy-start.3
  72.8 2.9 %copy.12 = bf16[256,2,8,128]{3,2,1,0:T(8,128)(2,1)} copy(bf16[256,2,8,128]{3,0,2,1:T(8,128)(2,1)} %bitcast.24) | data formatting | bytes 2097152
  75.7 0.0 copy-done.3
  75.7 0.0 copy-start.2
  75.7 0.9 %copy.13 = bf16[256,4,128]{2,1,0:T(4,128)(2,1)} copy(bf16[256,4,128]{2,0,1:T(8,128)(2,1)S(1)} %bitcast.31) | data formatting | bytes 524288
  76.6 0.0 copy-done.2
  76.7 0.9 %copy.14 = bf16[256,4,128]{2,1,0:T(4,128)(2,1)} copy(bf16[256,4,128]{2,0,1:T(8,128)(2,1)S(1)} %bitcast.30) | data formatting | bytes 524288
Async XLA Ops:
  0.6 3.1 %copy-start = (bf16[256,2,8,128]{3,2,1,0:T(8,128)(2,1)S(1)}, bf16[256,2,8,128]{3,2,1,0:T(8,128)(2,1)}, u32[]{:S(2)}) copy-start(bf16[256,2,8,128]{3,2,1,0:T(8,128)(2,1)} %param.8) | copy-start | bytes 3145732
  0.6 3.1 %copy-start.1 = (bf16[256,2,8,128]{3,2,1,0:T(8,128)(2,1)S(1)}, bf16[256,2,8,128]{3,2,1,0:T(8,128)(2,1)}, u32[]{:S(2)}) copy-start(bf16[256,2,8,128]{3,2,1,0:T(8,128)(2,1)} %param.5) | copy-start | bytes 3145732
  72.8 2.9 %copy-start.3 = (bf16[4,256,128]{2,1,0:T(8,128)(2,1)S(1)}, bf16[4,256,128]{2,1,0:T(8,128)(2,1)}, u32[]{:S(2)}) copy-start(bf16[4,256,128]{2,1,0:T(8,128)(2,1)} %get-tuple-element.21) | copy-start | bytes 786436
  75.7 1.0 %copy-start.2 = (bf16[4,256,128]{2,1,0:T(8,128)(2,1)S(1)}, bf16[4,256,128]{2,1,0:T(8,128)(2,1)}, u32[]{:S(2)}) copy-start(bf16[4,256,128]{2,1,0:T(8,128)(2,1)} %get-tuple-element.22) | copy-start | bytes 786436
